TPU v7x, 32 devices: a whole 2x2x4 slice. The times are simulated.
32 devices in a mesh: dp: 16 (over z, x, core), group: 2 (over y).
Axes of the slice: x: 2, y: 2, z: 4, core: 2. Of those that a mesh axis runs over, the one named last changes fastest.
Arguments:
- queries: bfloat16 [2048, 2, 2048], P('dp', None, 'group'), may hold values from -21 to 21
- new_keys: bfloat16 [2048, 2048], P('dp', 'group'), may hold values from -12 to 12
- new_values: bfloat16 [2048, 2048], P('dp', 'group'), may hold values from -6 to 6
- cache_keys: bfloat16 [16, 2048, 2048], P('dp', None, 'group'), may hold values from -6 to 6
- cache_values: bfloat16 [16, 2048, 2048], P('dp', None, 'group'), may hold values from -6 to 6
- lengths: int32 [16], P('dp'), may hold values from 1 to 2048, as said below
- att_gates: float32 [2048, 2], P('dp'), may hold values from 0.1 to 0.9
- resid: bfloat16 [2048, 2048], P('dp', 'group'), may hold values from -72 to 72
- norm_gain: float32 [2048], P('group'), may hold values from 0.5 to 1.5
- expert_ids: int32 [2048, 2], P('dp'), may hold values from 0 to 7, all different within a row; in each aligned block of 128 rows (0 to 127, 128 to 255, ...) at most 40 rows name the same one
- expert_gates: float32 [2048, 2], P('dp'), may hold values from 0.1 to 0.9
- w_gate: bfloat16 [16, 2048, 2816], P('dp', 'group'), may hold values from -0.125 to 0.125
- w_up: bfloat16 [16, 2048, 2816], P('dp', 'group'), may hold values from -0.125 to 0.125
- w_down: bfloat16 [16, 2816, 2048], P('dp', None, 'group'), may hold values from -0.078125 to 0.078125
Outputs:
- attended: bfloat16 [2048, 2048], P('dp', 'group')
- mixed: bfloat16 [2048, 2048], P('dp', 'group')
Inputs may be any that keep to these rules, and one draw needn't show every extreme that they name: `expert_ids`: in the tokens of one request (aligned blocks of 128 rows) no expert is named more than 40 times, a bound that some block reaches; the two experts of a row differ. `lengths`: some request has exactly 2048 cached tokens.
All inputs are finite; a program needn't handle non-finite values.
Results may differ from a plain program's by a relative error of at most 0.0055.
Values may be sent and summed in bfloat16 or wider, within the bound.
A program may use at most 128 MiB of HBM per device.

v0:
```python
import jax
import jax.numpy as jnp
from jax import lax
from jax.sharding import PartitionSpec as P

D = 2048
HD = 128
EXPERTS = 8
CACHE = 2048
CAP = 40


def pair_slots(expert_rows):
    flat_ids = expert_rows.reshape(-1)
    onehot = (flat_ids[:, None] == jnp.arange(EXPERTS, dtype=jnp.int32)[None, :]).astype(jnp.int32)
    running = jnp.cumsum(onehot, axis=0)
    return (jnp.sum(running * onehot, axis=1) - 1).reshape(expert_rows.shape)


def attend_local(queries, new_keys, new_values, cache_keys, cache_values, lengths, att_gates):
    row_count = queries.shape[0]
    local_heads = queries.shape[2] // HD
    query_h = queries.reshape(row_count, 2, local_heads, HD)
    key_new = new_keys.reshape(row_count, local_heads, HD)
    value_new = new_values.reshape(row_count, local_heads, HD)
    key_cache = cache_keys[0].reshape(CACHE, local_heads, HD)
    value_cache = cache_values[0].reshape(CACHE, local_heads, HD)
    length = lengths[0]
    score_scale = HD ** (-0.5)
    key_block = min(512, CACHE)
    blocks_live = (length + key_block - 1) // key_block

    def block_scores(block_index):
        keys_here = lax.dynamic_slice_in_dim(key_cache, block_index * key_block, key_block, 0)
        scores = (
            jnp.einsum("tshd,khd->shtk", query_h, keys_here, preferred_element_type=jnp.float32)
            * score_scale
        )
        position = block_index * key_block + jnp.arange(key_block, dtype=jnp.int32)
        return jnp.where(position[None, None, None, :] < length, scores, -jnp.inf)

    own_pos = jnp.arange(row_count, dtype=jnp.int32)
    causal = own_pos[None, :] <= own_pos[:, None]
    new_scores = (
        jnp.einsum("tshd,khd->shtk", query_h, key_new, preferred_element_type=jnp.float32)
        * score_scale
    )
    new_scores = jnp.where(causal[None, None], new_scores, -jnp.inf)
    row_max = jnp.max(new_scores, axis=-1)
    row_total = jnp.sum(jnp.exp(new_scores - row_max[..., None]), axis=-1)

    def stats_step(block_index, carry):
        old_max, old_total = carry
        scores = block_scores(block_index)
        new_max = jnp.maximum(old_max, jnp.max(scores, axis=-1))
        new_total = old_total * jnp.exp(old_max - new_max) + jnp.sum(
            jnp.exp(scores - new_max[..., None]), axis=-1
        )
        return (new_max, new_total)

    row_max, row_total = lax.fori_loop(0, blocks_live, stats_step, (row_max, row_total))

    def weigh(scores):
        return (jnp.exp(scores - row_max[..., None]) / row_total[..., None]).astype(jnp.bfloat16)

    output = jnp.einsum(
        "shtk,khd->tshd", weigh(new_scores), value_new, preferred_element_type=jnp.float32
    )

    def value_step(block_index, accum):
        values_here = lax.dynamic_slice_in_dim(value_cache, block_index * key_block, key_block, 0)
        return accum + jnp.einsum(
            "shtk,khd->tshd",
            weigh(block_scores(block_index)),
            values_here,
            preferred_element_type=jnp.float32,
        )

    output = lax.fori_loop(0, blocks_live, value_step, output)
    output = output.reshape(row_count, 2, local_heads * HD)
    return jnp.sum(output * att_gates[:, :, None], axis=1)


def on_device(
    queries,
    new_keys,
    new_values,
    cache_keys,
    cache_values,
    lengths,
    att_gates,
    resid,
    norm_gain,
    expert_ids,
    expert_gates,
    w_gate,
    w_up,
    w_down,
):
    row_count = queries.shape[0]
    attention = attend_local(
        queries, new_keys, new_values, cache_keys, cache_values, lengths, att_gates
    )
    attended = attention.astype(jnp.bfloat16)
    mixed_in = resid.astype(jnp.float32) + attention
    squares = lax.psum(jnp.sum(mixed_in * mixed_in, axis=1), "group")
    normed = (mixed_in / jnp.sqrt(squares[:, None] / D + 1e-05) * norm_gain[None, :]).astype(
        jnp.bfloat16
    )
    groups = lax.axis_size("group")
    owners = lax.axis_size("dp") // EXPERTS
    spread = owners * EXPERTS
    per_group = CAP // groups
    slot_index = pair_slots(expert_ids)
    slot_dest = expert_ids * CAP + slot_index
    slot_table = jnp.sum(
        (jnp.arange(EXPERTS * CAP, dtype=jnp.int32)[:, None, None] == slot_dest[None]).astype(
            jnp.bfloat16
        ),
        axis=2,
    )
    packed = jnp.dot(slot_table, normed, preferred_element_type=jnp.float32).astype(jnp.bfloat16)
    packed = packed.reshape(EXPERTS, 1, CAP, packed.shape[1])
    packed = jnp.broadcast_to(packed, (EXPERTS, owners, CAP, packed.shape[3])).reshape(
        spread, CAP, packed.shape[3]
    )
    arrived = lax.all_to_all(
        lax.all_to_all(packed, "dp", split_axis=0, concat_axis=0, tiled=True),
        "group",
        split_axis=1,
        concat_axis=2,
        tiled=True,
    )
    features = arrived.reshape(spread * per_group, arrived.shape[2])
    gate_act = jnp.dot(
        features,
        lax.all_gather(w_gate[0], "group", axis=0, tiled=True),
        preferred_element_type=jnp.float32,
    )
    up_act = jnp.dot(
        features,
        lax.all_gather(w_up[0], "group", axis=0, tiled=True),
        preferred_element_type=jnp.float32,
    )
    hidden = (jax.nn.silu(gate_act) * up_act).astype(jnp.bfloat16)
    partial_value = jnp.dot(
        hidden,
        lax.all_gather(w_down[0], "group", axis=1, tiled=True),
        preferred_element_type=jnp.float32,
    ).astype(jnp.bfloat16)
    partial_value = partial_value.reshape(spread, per_group, partial_value.shape[1])
    returned = lax.all_to_all(
        lax.all_to_all(partial_value, "dp", split_axis=0, concat_axis=0, tiled=True),
        "group",
        split_axis=2,
        concat_axis=1,
        tiled=True,
    )
    summed = jnp.sum(
        returned.reshape(EXPERTS, owners, CAP, returned.shape[2]).astype(jnp.float32), axis=1
    )
    summed = summed.reshape(EXPERTS * CAP, returned.shape[2])
    picked = jnp.take(summed, slot_dest.reshape(-1), axis=0).reshape(row_count, 2, summed.shape[1])
    expert_mix = jnp.sum(picked * expert_gates[:, :, None], axis=1)
    mixed = (mixed_in + expert_mix).astype(jnp.bfloat16)
    return (attended, mixed)


def solution(mesh):
    in_specs = (
        P("dp", None, "group"),
        P("dp", "group"),
        P("dp", "group"),
        P("dp", None, "group"),
        P("dp", None, "group"),
        P("dp"),
        P("dp", None),
        P("dp", "group"),
        P("group"),
        P("dp", None),
        P("dp", None),
        P("dp", "group", None),
        P("dp", "group", None),
        P("dp", None, "group"),
    )
    out_specs = (P("dp", "group"), P("dp", "group"))
    return jax.shard_map(
        on_device, mesh=mesh, in_specs=in_specs, out_specs=out_specs, check_vma=False
    )
```

profile of v0, /device:TPU:0, one launch (start us, length us, event | category | flops | bytes accessed | tf_op | source)
XLA Modules:
  0.0 622.0 jit_solution(718074174924362139)
XLA Ops:
  11.0 6.5 %copy.120 = bf16[1,2048,1024]{1,2,0:T(8,128)(2,1)} copy(bf16[1,2048,1024]{2,1,0:T(8,128)(2,1)} %param.21) | data formatting | bytes 8388608 | tf_op args[3]
  17.5 6.9 %copy.121 = bf16[2048,8,128]{2,0,1:T(8,128)(2,1)} copy(bf16[2048,8,128]{0,2,1:T(8,128)(2,1)} %bitcast.146) | data formatting | bytes 8388608 | tf_op jit(solution)/shard_map/while | solution.py:61
  24.9 11.2 %while.22 = (s32[]{:T(128)}, f32[2,8,128]{2,0,1:T(2,128)S(1)}, f32[2,8,128]{2,0,1:T(2,128)S(1)}, s32[]{:T(128)}, s32[]{:T(128)}, /*index=5*/bf16[2048,8,128]{2,0...) while((s32[]{:T(128)}, f32[2,8,128]{2,0,1:T(2,128)S(1)}, ...), condition=%wide.region_5.6_spmd, body=%wide.region_2.5_spmd.sunk | while | flops 275780608 | bytes 10069671 | solution.py:61
  37.3 6.5 %copy.125 = bf16[1,2048,1024]{1,2,0:T(8,128)(2,1)} copy(bf16[1,2048,1024]{2,1,0:T(8,128)(2,1)} %param.22) | data formatting | bytes 8388608 | tf_op args[4]
  43.8 11.5 %while.23 = (s32[]{:T(128)}, f32[128,2,8,128]{0,3,1,2:T(8,128)S(1)}, s32[]{:T(128)}, bf16[2048,8,128]{0,2,1:T(8,128)(2,1)}, s32[]{:T(128)}, /*index=5*/bf16[2048...) while((s32[]{:T(128)}, ...), condition=%wide.region_7.8_spmd, body=%wide.region_6.7_spmd.sunk | while | flops 542376960 | bytes 4737203 | solution.py:79
  44.6 3.1 fusion.70
  52.2 3.1 fusion.70
  57.0 5.9 psum.7
  63.5 45.1 %all_to_all.34 = bf16[16,40,1024]{2,1,0:T(8,128)(2,1)S(1)} all-to-all(bf16[16,40,1024]{2,1,0:T(8,128)(2,1)S(1)} %bitcast.148), channel_id=1, replica_groups=mesh['dp'=16,'group'=2] {'dp'}, dimensions={0} | all-to-all | bytes 2621440 | tf_op jit(solution)/shard_map/all_to_all | solution.py:128
  109.4 34.5 %all_to_all.35 = bf16[16,40,1024]{2,0,1:T(8,128)(2,1)S(1)} all-to-all(bf16[16,40,1024]{2,0,1:T(8,128)(2,1)S(1)} %copy.135), channel_id=1, replica_groups=mesh['dp'=16,'group'=2] {'group'}, dimensions={1} | all-to-all | bytes 2621440 | tf_op jit(solution)/shard_map/all_to_all | solution.py:127
  145.6 21.8 %all-gather.7.cloned.1.call-done = bf16[1,2048,2816]{2,1,0:T(8,128)(2,1)} async-done(((bf16[1,1024,2816]{2,1,0:T(8,128)(2,1)}), bf16[1,2048,2816]{2,1,0:T(8,128)(2,1)}) %all-gather.7.cloned.1.call-update) | async-done | bytes 11534352 | tf_op jit(solution)/shard_map/all_gather | solution.py:137
  167.4 8.7 %fusion.26 = f32[320,2816]{1,0:T(8,128)} fusion(bf16[320,2048]{1,0:T(8,128)(2,1)S(1)} %bitcast.156, bf16[1,2048,2816]{2,1,0:T(8,128)(2,1)} %all-gather.7.cloned.1.call-done), kind=kOutput, calls=%fused_computation.31 | convolution fusion | flops 3690987520 | bytes 16449536 | tf_op jit(solution)/shard_map/dot_general | solution.py:135
  176.1 133.9 %all-gather.11.cloned.1.call-done = bf16[1,2816,2048]{2,1,0:T(8,128)(2,1)} async-done(((bf16[1,2816,1024]{2,1,0:T(8,128)(2,1)}), bf16[1,2816,2048]{2,1,0:T(8,128)(2,1)}) %all-gather.11.cloned.1.call-update) | async-done | bytes 11534352 | tf_op jit(solution)/shard_map/all_gather | solution.py:148
  310.0 142.6 %all-gather.9.cloned.1.call-done = bf16[1,2048,2816]{2,1,0:T(8,128)(2,1)} async-done(((bf16[1,1024,2816]{2,1,0:T(8,128)(2,1)}), bf16[1,2048,2816]{2,1,0:T(8,128)(2,1)}) %all-gather.9.cloned.1.call-update) | async-done | bytes 11534352 | tf_op jit(solution)/shard_map/all_gather | solution.py:142
  452.7 17.4 %fusion.34 = bf16[320,2048]{1,0:T(8,128)(2,1)} fusion(bf16[1,2816,2048]{2,1,0:T(8,128)(2,1)} %all-gather.11.cloned.1.call-done, bf16[320,2048]{1,0:T(8,128)(2,1)S(1)} %bitcast.157, bf16[1,2048,2816]{2,1,0:T(8,128)(2,1)} %all-gather.9.cloned.1.call-done, f32[320,2816]{1,0:T(8,128)} %fusion.26), kind=kOutput, calls=%fused_computation.35 | convolution fusion | flops 7388037120 | bytes 29294592 | tf_op jit(solution)/shard_map/dot_general | solution.py:146
  472.3 41.9 %all_to_all.36 = bf16[16,20,2048]{2,1,0:T(8,128)(2,1)S(1)} all-to-all(bf16[16,20,2048]{2,1,0:T(8,128)(2,1)S(1)} %reshape.145), channel_id=1, replica_groups=mesh['dp'=16,'group'=2] {'dp'}, dimensions={0} | all-to-all | bytes 2621440 | tf_op jit(solution)/shard_map/all_to_all | solution.py:153
  514.2 8.9 %copy.137 = bf16[16,20,2048]{1,0,2:T(8,128)(2,1)} copy(bf16[16,20,2048]{2,1,0:T(8,128)(2,1)S(1)} %all_to_all.36) | data formatting | bytes 2621440 | tf_op jit(solution)/shard_map/all_to_all | solution.py:153
  523.1 22.2 %reshape.167 = bf16[2,2,163840]{2,1,0:T(2,128)(2,1)} reshape(bf16[2048,16,20]{2,1,0:T(8,128)(2,1)} %bitcast.144) | data formatting | bytes 2621440
  545.2 3.8 all-to-all-start.3
  549.6 17.0 %all-to-all-done.3 = bf16[2,2,163840]{2,1,0:T(2,128)(2,1)S(1)} async-done(((bf16[2,2,163840]{2,1,0:T(2,128)(2,1)}), bf16[2,2,163840]{2,1,0:T(2,128)(2,1)S(1)}, u32[]{:S(2)}, u32[]{:S(2)}) %all-to-all-start.3) | async-done | bytes 1310752 | tf_op jit(solution)/shard_map/all_to_all | solution.py:152
  566.6 23.9 %reshape.168 = bf16[2048,16,20]{2,1,0:T(8,128)(2,1)} reshape(bf16[2,2,163840]{2,1,0:T(2,128)(2,1)S(1)} %all-to-all-done.3) | data formatting | bytes 2621440
  590.5 10.3 %copy.138 = bf16[16,20,2048]{2,0,1:T(8,128)(2,1)} copy(bf16[16,20,2048]{1,0,2:T(8,128)(2,1)} %bitcast.145) | data formatting | bytes 2621440 | tf_op jit(solution)/shard_map/all_to_all | solution.py:152
  600.8 3.8 reshape.149
  604.6 3.9 reduce.2
  (93 shorter events, 34.9 us)
Async XLA Ops:
  7.2 160.3 %all-gather.7.cloned.1.call-start = ((), (), s32[]{:S(2)}) async-start(), calls=%async_computation.4 | async-start | bytes 17301504 | tf_op jit(solution)/shard_map/all_gather | solution.py:137
  7.9 302.2 %all-gather.11.cloned.1.call-start = ((), (), s32[]{:S(2)}) async-start(), calls=%async_computation.6 | async-start | bytes 17301504 | tf_op jit(solution)/shard_map/all_gather | solution.py:148
  8.6 1.4 copy-start.3
  8.7 2.3 copy-start.4
  8.7 444.0 %all-gather.9.cloned.1.call-start = ((), (), s32[]{:S(2)}) async-start(), calls=%async_computation.5 | async-start | bytes 17301504 | tf_op jit(solution)/shard_map/all_gather | solution.py:142
  24.9 11.2 %copy-start.6 = (s32[128,2]{0,1:T(2,128)S(1)}, s32[128,2]{0,1:T(2,128)}, u32[]{:S(2)}) copy-start(s32[128,2]{0,1:T(2,128)} %param.27) | copy-start | bytes 3076
  24.9 11.6 %copy-start.5 = (bf16[128,1024]{1,0:T(8,128)(2,1)S(1)}, bf16[128,1024]{1,0:T(8,128)(2,1)}, u32[]{:S(2)}) copy-start(bf16[128,1024]{1,0:T(8,128)(2,1)} %param.20) | copy-start | bytes 786436
  43.8 11.5 %copy-start.8 = (f32[128,2]{0,1:T(2,128)S(1)}, f32[128,2]{0,1:T(2,128)}, u32[]{:S(2)}) copy-start(f32[128,2]{0,1:T(2,128)} %param.24) | copy-start | bytes 3076
  43.8 13.0 %copy-start.2 = (bf16[128,1024]{1,0:T(8,128)(2,1)S(1)}, bf16[128,1024]{1,0:T(8,128)(2,1)}, u32[]{:S(2)}) copy-start(bf16[128,1024]{1,0:T(8,128)(2,1)} %param.25) | copy-start | bytes 786436
  43.8 19.1 %copy-start.9 = (f32[1024]{0:T(1024)S(1)}, f32[1024]{0:T(1024)}, u32[]{:S(2)}) copy-start(f32[1024]{0:T(1024)} %param.26) | copy-start | bytes 12292
  55.6 53.7 %copy-start = (f32[128,1024]{1,0:T(8,128)}, f32[128,1024]{1,0:T(8,128)S(1)}, u32[]{:S(2)}) copy-start(f32[128,1024]{1,0:T(8,128)S(1)} %copy.129) | copy-start | bytes 1572868
  523.1 26.4 %copy-start.7 = (f32[128,2]{0,1:T(2,128)S(1)}, f32[128,2]{0,1:T(2,128)}, u32[]{:S(2)}) copy-start(f32[128,2]{0,1:T(2,128)} %param.28) | copy-start | bytes 3076
  545.2 21.4 %all-to-all-start.3 = ((bf16[2,2,163840]{2,1,0:T(2,128)(2,1)}), bf16[2,2,163840]{2,1,0:T(2,128)(2,1)S(1)}, u32[]{:S(2)}, u32[]{:S(2)}) async-start(bf16[2,2,163840]{2,1,0:T(2,128)(2,1)} %reshape.167), calls=%async_computation.3 | async-start | bytes 2621440 | tf_op jit(solution)/shard_map/all_to_all | solution.py:152
  611.0 3.3 copy-start.1
Sparse Core Ops, SparseCore 0:
  9.6 157.8 all-gather.6
  169.0 141.0 all-gather.10
  311.6 141.0 all-gather.8
where the time goes:
time: 630 us; the launch traced here: 622 us
  waiting for transfers between devices  318 us (50%)
  blocking collectives  127 us (20%)
  local copies, waits for them, and re-layouts  101 us (16%)
  matrix products  42.7 us (7%)
  between operations  15 us (2%)
  other arithmetic  14.5 us (2%)
    all_gather x1, waiting for transfers between devices, on_device(): lax.all_gather(w_up[0], 'group', axis=0, tiled=True)  143 us
    all_gather x1, waiting for transfers between devices, on_device(): lax.all_gather(w_down[0], 'group', axis=1, tiled=True)  134 us
    unnamed x31, local copies, waits for them, and re-layouts  62 us
    all_to_all x1, blocking collectives, on_device(): lax.all_to_all(packed, 'dp', split_axis=0, concat_axis=0, tiled=True)  45.1 us
    all_to_all x1, blocking collectives, on_device(): lax.all_to_all(partial_value, 'dp', split_axis=0, concat_axis=0, tiled=True)  41.9 us
    all_to_all x1, blocking collectives, on_device(): lax.all_to_all(lax.all_to_all(packed, 'dp', split_axis=0, concat_axis=0,...  34.5 us
    all_gather x1, waiting for transfers between devices, on_device(): lax.all_gather(w_gate[0], 'group', axis=0, tiled=True)  21.8 us
    dot_general x1, matrix products, on_device(): jnp.dot(hidden, lax.all_gather(w_down[0], 'group', axis=1, tiled=True), p...  17.4 us
  transfers between devices with their start and end apart: 4, of which 4 were waited for; matrix products, arithmetic and copies ran while one was open for 9% of the time, Pallas kernels for 0%

commit v1 on v0

v1 whole, which is shorter than its diff:
```python
import functools
import math

import jax
import jax.numpy as jnp
from jax import lax
from jax.experimental import pallas as pl
from jax.experimental.pallas import tpu as pltpu
from jax.sharding import PartitionSpec as P

D = 2048
HD = 128
EXPERTS = 8
CACHE = 2048
CAP = 40


def pair_slots(expert_rows):
    flat_ids = expert_rows.reshape(-1)
    onehot = (flat_ids[:, None] == jnp.arange(EXPERTS, dtype=jnp.int32)[None, :]).astype(jnp.int32)
    running = jnp.cumsum(onehot, axis=0)
    return (jnp.sum(running * onehot, axis=1) - 1).reshape(expert_rows.shape)


def attend_kernel(
    len_ref, query_ref, key_new_ref, value_new_ref, key_ref, value_ref, gate_ref, resid_ref,
    attended_ref, mixed_ref, square_ref,
):
    row_count = key_new_ref.shape[0]
    cache = key_ref.shape[1]
    factor = HD ** (-0.5) * math.log2(math.e)
    contract_last = (((1,), (1,)), ((), ()))
    query = query_ref[...]
    scores = lax.dot_general(
        query, key_ref[0], contract_last, preferred_element_type=jnp.float32
    )
    position = lax.broadcasted_iota(jnp.int32, (1, cache), 1)
    scores = jnp.where(position < len_ref[0], scores, -jnp.inf)
    new_scores = lax.dot_general(
        query, key_new_ref[...], contract_last, preferred_element_type=jnp.float32
    )
    token = lax.rem(lax.broadcasted_iota(jnp.int32, new_scores.shape, 0), row_count)
    own = lax.broadcasted_iota(jnp.int32, new_scores.shape, 1)
    new_scores = jnp.where(own <= token, new_scores, -jnp.inf)
    row_max = jnp.maximum(
        jnp.max(scores, axis=1, keepdims=True), jnp.max(new_scores, axis=1, keepdims=True)
    )
    probs = jnp.exp2((scores - row_max) * factor)
    new_probs = jnp.exp2((new_scores - row_max) * factor)
    total = jnp.sum(probs, axis=1, keepdims=True) + jnp.sum(new_probs, axis=1, keepdims=True)
    output = jnp.dot(
        probs.astype(jnp.bfloat16), value_ref[0], preferred_element_type=jnp.float32
    ) + jnp.dot(
        new_probs.astype(jnp.bfloat16), value_new_ref[...], preferred_element_type=jnp.float32
    )
    output = output * (gate_ref[...] / total)
    attention = output[:row_count] + output[row_count:]
    attended_ref[...] = attention.astype(attended_ref.dtype)
    mixed_in = resid_ref[...].astype(jnp.float32) + attention
    mixed_ref[...] = mixed_in

    @pl.when(pl.program_id(0) == 0)
    def _():
        square_ref[...] = jnp.zeros_like(square_ref)

    square_ref[...] += mixed_in * mixed_in


def attend_local(
    queries, new_keys, new_values, cache_keys, cache_values, lengths, att_gates, resid
):
    row_count, _, width = queries.shape
    heads = width // HD
    cache = cache_keys.shape[1]
    query_rows = jnp.transpose(queries, (1, 0, 2)).reshape(2 * row_count, width)
    gate_rows = jnp.transpose(att_gates, (1, 0)).reshape(2 * row_count, 1)
    rows = pl.BlockSpec((row_count, HD), lambda h: (0, h))
    cached = pl.BlockSpec((1, cache, HD), lambda h: (0, 0, h))
    score_count = 2 * row_count * (cache + row_count) * heads
    return pl.pallas_call(
        attend_kernel,
        grid=(heads,),
        in_specs=[
            pl.BlockSpec(memory_space=pltpu.SMEM),
            pl.BlockSpec((2 * row_count, HD), lambda h: (0, h)),
            rows,
            rows,
            cached,
            cached,
            pl.BlockSpec((2 * row_count, 1), lambda h: (0, 0)),
            rows,
        ],
        out_specs=[rows, rows, pl.BlockSpec((row_count, HD), lambda h: (0, 0))],
        out_shape=[
            jax.ShapeDtypeStruct((row_count, width), jnp.bfloat16),
            jax.ShapeDtypeStruct((row_count, width), jnp.float32),
            jax.ShapeDtypeStruct((row_count, HD), jnp.float32),
        ],
        compiler_params=pltpu.CompilerParams(vmem_limit_bytes=40 * 1024 * 1024),
        cost_estimate=pl.CostEstimate(
            flops=4 * score_count * HD,
            bytes_accessed=4 * cache * width,
            transcendentals=score_count,
        ),
    )(lengths, query_rows, new_keys, new_values, cache_keys, cache_values, gate_rows, resid)


def experts_gathered(normed, expert_ids, slot_index, expert_gates, w_gate, w_up, w_down):
    row_count = normed.shape[0]
    groups = lax.axis_size("group")
    owners = lax.axis_size("dp") // EXPERTS
    spread = owners * EXPERTS
    per_group = CAP // groups
    slot_dest = expert_ids * CAP + slot_index
    slot_table = jnp.sum(
        (jnp.arange(EXPERTS * CAP, dtype=jnp.int32)[:, None, None] == slot_dest[None]).astype(
            jnp.bfloat16
        ),
        axis=2,
    )
    packed = jnp.dot(slot_table, normed, preferred_element_type=jnp.float32).astype(jnp.bfloat16)
    packed = packed.reshape(EXPERTS, 1, CAP, packed.shape[1])
    packed = jnp.broadcast_to(packed, (EXPERTS, owners, CAP, packed.shape[3])).reshape(
        spread, CAP, packed.shape[3]
    )
    arrived = lax.all_to_all(
        lax.all_to_all(packed, "dp", split_axis=0, concat_axis=0, tiled=True),
        "group",
        split_axis=1,
        concat_axis=2,
        tiled=True,
    )
    features = arrived.reshape(spread * per_group, arrived.shape[2])
    gate_act = jnp.dot(
        features,
        lax.all_gather(w_gate[0], "group", axis=0, tiled=True),
        preferred_element_type=jnp.float32,
    )
    up_act = jnp.dot(
        features,
        lax.all_gather(w_up[0], "group", axis=0, tiled=True),
        preferred_element_type=jnp.float32,
    )
    hidden = (jax.nn.silu(gate_act) * up_act).astype(jnp.bfloat16)
    partial_value = jnp.dot(
        hidden,
        lax.all_gather(w_down[0], "group", axis=1, tiled=True),
        preferred_element_type=jnp.float32,
    ).astype(jnp.bfloat16)
    partial_value = partial_value.reshape(spread, per_group, partial_value.shape[1])
    returned = lax.all_to_all(
        lax.all_to_all(partial_value, "dp", split_axis=0, concat_axis=0, tiled=True),
        "group",
        split_axis=2,
        concat_axis=1,
        tiled=True,
    )
    summed = jnp.sum(
        returned.reshape(EXPERTS, owners, CAP, returned.shape[2]).astype(jnp.float32), axis=1
    )
    summed = summed.reshape(EXPERTS * CAP, returned.shape[2])
    picked = jnp.take(summed, slot_dest.reshape(-1), axis=0).reshape(row_count, 2, summed.shape[1])
    return jnp.sum(picked * expert_gates[:, :, None], axis=1)


CHUNKS = ((0, 16), (16, 24))


def dot32(left, right):
    return jnp.dot(left, right, preferred_element_type=jnp.float32)


def experts_paired(normed, expert_ids, slot_index, expert_gates, w_gate, w_up, w_down):
    width = normed.shape[1]
    dp = lax.axis_size("dp")
    blocks = dp // 2
    first_group = lax.axis_index("group") == 0
    same_owner = [list(range(j, dp, 2)) for j in range(2)]
    swap_owner = [(i, i + 1 - 2 * (i % 2)) for i in range(dp)]
    swap_group = [(0, 1), (1, 0)]

    def exchange(rows):
        return lax.all_to_all(
            rows.reshape(EXPERTS, -1, width), "dp", split_axis=0, concat_axis=0,
            axis_index_groups=same_owner, tiled=True,
        ).reshape(-1, width)

    def slots_onehot(first, count):
        inside = (slot_index >= first) & (slot_index < first + count)
        dest = jnp.where(inside, expert_ids * count + slot_index - first, -1)
        return (
            jnp.arange(EXPERTS * count, dtype=jnp.int32)[None, :, None] == dest[:, None, :]
        ).astype(jnp.bfloat16)

    mix = 0.0
    before = None
    stages = []
    for first, count in CHUNKS:
        onehot = slots_onehot(first, count)
        table = jnp.sum(onehot, axis=2)
        packed = lax.dot_general(
            table, normed, (((0,), (0,)), ((), ())), preferred_element_type=jnp.float32
        ).astype(jnp.bfloat16)
        if before is not None:
            packed, before[0], before[1] = lax.optimization_barrier(
                (packed, before[0], before[1])
            )
        own = exchange(packed)
        other = lax.ppermute(own, "dp", swap_owner)
        keep = jnp.where(first_group, own, other)
        send = jnp.where(first_group, other, own)
        before = [
            dot32(send, w_gate).astype(jnp.bfloat16),
            dot32(send, w_up).astype(jnp.bfloat16),
        ]
        stages.append((onehot, keep, before))
    for onehot, keep, sent in stages:
        gate_act = dot32(keep, w_gate) + lax.ppermute(sent[0], "group", swap_group)
        up_act = dot32(keep, w_up) + lax.ppermute(sent[1], "group", swap_group)
        hidden_keep = (jax.nn.silu(gate_act) * up_act).astype(jnp.bfloat16)
        hidden_send = lax.ppermute(hidden_keep, "group", swap_group)
        part_keep = dot32(hidden_keep, w_down).astype(jnp.bfloat16)
        part_send = dot32(hidden_send, w_down).astype(jnp.bfloat16)
        part_own = jnp.where(first_group, part_keep, part_send)
        part_other = jnp.where(first_group, part_send, part_keep)
        summed = part_own.astype(jnp.float32) + lax.ppermute(
            part_other, "dp", swap_owner
        ).astype(jnp.float32)
        returned = exchange(summed.astype(jnp.bfloat16))
        for k in range(2):
            mix = mix + dot32(onehot[:, :, k], returned) * expert_gates[:, k : k + 1]
    return mix


def on_device(
    queries,
    new_keys,
    new_values,
    cache_keys,
    cache_values,
    lengths,
    att_gates,
    resid,
    norm_gain,
    expert_ids,
    expert_gates,
    w_gate,
    w_up,
    w_down,
):
    row_count = queries.shape[0]
    attended, mixed_in, squares = attend_local(
        queries, new_keys, new_values, cache_keys, cache_values, lengths, att_gates, resid
    )
    squares = lax.psum(jnp.sum(squares, axis=1), "group")
    normed = (mixed_in / jnp.sqrt(squares[:, None] / D + 1e-05) * norm_gain[None, :]).astype(
        jnp.bfloat16
    )
    slot_index = pair_slots(expert_ids)
    owners = lax.axis_size("dp") // EXPERTS
    if lax.axis_size("group") == 2 and owners == 2:
        expert_mix = experts_paired(
            normed, expert_ids, slot_index, expert_gates, w_gate[0], w_up[0], w_down[0]
        )
    else:
        expert_mix = experts_gathered(
            normed, expert_ids, slot_index, expert_gates, w_gate, w_up, w_down
        )
    mixed = (mixed_in + expert_mix).astype(jnp.bfloat16)
    return (attended, mixed)


def solution(mesh):
    in_specs = (
        P("dp", None, "group"),
        P("dp", "group"),
        P("dp", "group"),
        P("dp", None, "group"),
        P("dp", None, "group"),
        P("dp"),
        P("dp", None),
        P("dp", "group"),
        P("group"),
        P("dp", None),
        P("dp", None),
        P("dp", "group", None),
        P("dp", "group", None),
        P("dp", None, "group"),
    )
    out_specs = (P("dp", "group"), P("dp", "group"))
    return jax.shard_map(
        on_device, mesh=mesh, in_specs=in_specs, out_specs=out_specs, check_vma=False
    )
```

time: 630 us -> 206 us (0.33); the launches traced: 622 us -> 205 us
  waiting for transfers between devices: 318 us -> 111 us
  blocking collectives: 127 us -> 20.2 us
  local copies, waits for them, and re-layouts: 101 us -> 10.7 us
  matrix products: 42.7 us -> 26.7 us
  starting transfers between devices: 3.91 us -> 18.2 us
  Pallas kernels: 0 us -> 13.5 us
  between operations: 15 us -> 1.64 us
  other arithmetic: 14.5 us -> 3.72 us
    all_gather x3 -> x0, waiting for transfers between devices: 298 us -> none  [the longest x1 143 us: on_device(): lax.all_gather(w_up[0], 'group', axis=0, tiled=True)]
    all_to_all x3 -> x1, blocking collectives: 122 us -> 14.4 us  [exchange(): lax.all_to_all(rows.reshape(EXPERTS, -1, width), 'dp', split_axis=0, conc...]
    ppermute x0 -> x10, waiting for transfers between devices: none -> 79 us  [the longest x2 31.8 us: experts_paired(): hidden_send = lax.ppermute(hidden_keep, 'group', swap_group)]
    unnamed x31 -> x29, local copies, waits for them, and re-layouts: 62 us -> 8.07 us
    all_to_all x4 -> x0, local copies, waits for them, and re-layouts: 21.2 us -> none  [the longest x1 10.3 us: on_device(): lax.all_to_all(lax.all_to_all(partial_value, 'dp', split_axis=0, concat_a...]
    dot_general x11 -> x18, matrix products: 42.7 us -> 26.7 us  [the longest x16 25.4 us: dot32(): return jnp.dot(left, right, preferred_element_type=jnp.float32)]
    all_to_all x1 -> x3, waiting for transfers between devices: 17 us -> 31.6 us  [exchange(): lax.all_to_all(rows.reshape(EXPERTS, -1, width), 'dp', split_axis=0, conc...]
    pallas_call x0 -> x1, Pallas kernels: none -> 13.5 us  [attend_local(): pl.pallas_call(attend_kernel, grid=(heads,), in_specs=[pl.BlockSpec(memor...]
  transfers between devices with their start and end apart: 4 -> 13, of which waited for: 4 -> 10; matrix products, arithmetic and copies ran while one was open for 9% -> 11% of each run, Pallas kernels for 0% -> 0%
where the time goes in v1:
time: 206 us; the launch traced here: 205 us
  waiting for transfers between devices  111 us (54%)
  matrix products  26.7 us (13%)
  blocking collectives  20.2 us (10%)
  starting transfers between devices  18.2 us (9%)
  Pallas kernels  13.5 us (7%)
  local copies, waits for them, and re-layouts  10.7 us (5%)
  other arithmetic  3.72 us (2%)
    ppermute x2, waiting for transfers between devices, experts_paired(): hidden_send = lax.ppermute(hidden_keep, 'group', swap_group)  31.8 us
    all_to_all x3, waiting for transfers between devices, exchange(): lax.all_to_all(rows.reshape(EXPERTS, -1, width), 'dp', split_axis=0, conc...  31.6 us
    ppermute x2, waiting for transfers between devices, experts_paired(): up_act = dot32(keep, w_up) + lax.ppermute(sent[1], 'group', swap_group)  25.9 us
    dot_general x16, matrix products, dot32(): return jnp.dot(left, right, preferred_element_type=jnp.float32)  25.4 us
    ppermute x2, waiting for transfers between devices, experts_paired(): gate_act = dot32(keep, w_gate) + lax.ppermute(sent[0], 'group', swap_group)  20.9 us
    all_to_all x1, blocking collectives, exchange(): lax.all_to_all(rows.reshape(EXPERTS, -1, width), 'dp', split_axis=0, conc...  14.4 us
    pallas_call x1, Pallas kernels, attend_local(): pl.pallas_call(attend_kernel, grid=(heads,), in_specs=[pl.BlockSpec(memor...  13.5 us
    all_to_all x3, starting transfers between devices, exchange(): lax.all_to_all(rows.reshape(EXPERTS, -1, width), 'dp', split_axis=0, conc...  10.6 us
  transfers between devices with their start and end apart: 13, of which 10 were waited for; matrix products, arithmetic and copies ran while one was open for 11% of the time, Pallas kernels for 0%

profile of v1, /device:TPU:0, one launch (start us, length us, event | category | flops | bytes accessed | tf_op | source)
XLA Modules:
  0.0 205.4 jit_solution(10799492937322413802)
XLA Ops:
  6.2 2.2 %copy-done = bf16[1,2048,1024]{2,1,0:T(8,128)(2,1)S(1)} copy-done((bf16[1,2048,1024]{2,1,0:T(8,128)(2,1)S(1)}, bf16[1,2048,1024]{2,1,0:T(8,128)(2,1)}, u32[]{:S(2)}) %copy-start) | copy-done | bytes 4194328
  8.4 2.2 %copy-done.1 = bf16[1,2048,1024]{2,1,0:T(8,128)(2,1)S(1)} copy-done((bf16[1,2048,1024]{2,1,0:T(8,128)(2,1)S(1)}, bf16[1,2048,1024]{2,1,0:T(8,128)(2,1)}, u32[]{:S(2)}) %copy-start.1) | copy-done | bytes 4194328
  13.4 13.5 %shard_map.149 = (bf16[128,1024]{1,0:T(8,128)(2,1)}, f32[128,1024]{1,0:T(8,128)S(1)}, f32[128,128]{1,0:T(8,128)S(1)}) custom-call(s32[1]{0:T(128)S(6)} %copy.51.len_ref, bf16[256,1024]{1,0:T(8,128)(2,1)S(1)} %bitcast.106, bf16[128,1024]{1,0:T(8,128)(2,1)S(1)} %copy-done.2, bf16[128,1024]{1,0:T(8,128)(2,1)S(1)} %copy-done.3, ...), custom_call_target="tpu_custom_call" | custom-call | flops 2281701376 | bytes 8388608 | tf_op jit(solution)/shard_map/pallas_call | solution.py:80
  27.1 5.9 %psum.7 = f32[128]{0:T(128)S(1)} all-reduce(f32[128]{0:T(128)S(1)} %reduce_sum.44), channel_id=1, replica_groups=mesh['dp'=16,'group'=2] {'group'}, use_global_device_ids=true, to_apply=%region_5.6 | all-reduce | flops 128 | bytes 1024 | tf_op jit(solution)/shard_map/psum | solution.py:255
  33.5 14.4 %all_to_all.20 = bf16[8,16,1024]{2,1,0:T(8,128)(2,1)S(1)} all-to-all(bf16[8,16,1024]{2,1,0:T(8,128)(2,1)S(1)} %bitcast.127), channel_id=1, replica_groups={{0,4,8,12,16,20,24,28},{2,6,10,14,18,22,26,30},{1,5,9,13,17,21,25,29},{..., dimensions={0} | all-to-all | bytes 524288 | tf_op jit(solution)/shard_map/all_to_all | solution.py:183
  49.4 3.8 %fusion.42 = bf16[128,2816]{1,0:T(8,128)(2,1)S(1)} fusion(bf16[1,1024,2816]{2,1,0:T(8,128)(2,1)} %param.25, bf16[128,1024]{1,0:T(8,128)(2,1)S(1)} %collective-permute-done, bf16[128,1024]{1,0:T(8,128)(2,1)S(1)} %bitcast.119, pred[]{:T(512)S(6)} %eq.65), kind=kOutput, calls=%fused_computation.30 | convolution fusion | flops 738689024 | bytes 7012353 | tf_op jit(solution)/shard_map/dot_general | solution.py:170
  54.1 1.6 collective-permute-start.1
  55.7 3.6 %all-to-all-start.2 = ((bf16[8,24,1024]{2,1,0:T(8,128)(2,1)}), bf16[8,24,1024]{2,1,0:T(8,128)(2,1)S(1)}, u32[]{:S(2)}, u32[]{:S(2)}) async-start(bf16[8,24,1024]{2,1,0:T(8,128)(2,1)} %bitcast.18), calls=%async_computation.2 | async-start | bytes 786432 | tf_op jit(solution)/shard_map/all_to_all | solution.py:183
  60.0 11.5 %all-to-all-done.2 = bf16[8,24,1024]{2,1,0:T(8,128)(2,1)S(1)} async-done(((bf16[8,24,1024]{2,1,0:T(8,128)(2,1)}), bf16[8,24,1024]{2,1,0:T(8,128)(2,1)S(1)}, u32[]{:S(2)}, u32[]{:S(2)}) %all-to-all-start.2) | async-done | bytes 393248 | tf_op jit(solution)/shard_map/all_to_all | solution.py:183
  71.5 1.8 collective-permute-done.1
  73.2 3.9 %fusion.36 = f32[128,2816]{1,0:T(8,128)S(1)} fusion(bf16[1,1024,2816]{2,1,0:T(8,128)(2,1)} %param.25, bf16[128,2816]{1,0:T(8,128)(2,1)} %collective-permute-done.1, bf16[128,1024]{1,0:T(8,128)(2,1)S(1)} %bitcast.121, bf16[128,1024]{1,0:T(8,128)(2,1)S(1)} %collective-permute-done, pred[]{:T(512)S(6)} %eq.65), kind=kOutput, calls=%fused_computation.28 | convolution fusion | flops 739049472 | bytes 8454145 | tf_op jit(solution)/shard_map/dot_general | solution.py:170
  78.5 1.6 collective-permute-start.6
  80.1 3.9 %fusion.33 = bf16[192,2816]{1,0:T(8,128)(2,1)S(1)} fusion(bf16[1,1024,2816]{2,1,0:T(8,128)(2,1)} %param.26, bf16[192,1024]{1,0:T(8,128)(2,1)S(1)} %collective-permute-done.5, bf16[192,1024]{1,0:T(8,128)(2,1)S(1)} %bitcast.115, pred[]{:T(512)S(6)} %eq.65), kind=kOutput, calls=%fused_computation.27 | convolution fusion | flops 1108033536 | bytes 7634945 | tf_op jit(solution)/shard_map/dot_general | solution.py:170
  84.6 4.1 %collective-permute-done.2 = bf16[128,2816]{1,0:T(8,128)(2,1)} collective-permute-done((bf16[128,2816]{1,0:T(8,128)(2,1)S(1)}, bf16[128,2816]{1,0:T(8,128)(2,1)}, u32[]{:S(2)}, u32[]{:S(2)}) %collective-permute-start.2) | collective-permute-done | bytes 720928 | tf_op jit(solution)/shard_map/ppermute | solution.py:219
  88.7 2.4 %multiply_convert_fusion.1 = bf16[128,2816]{1,0:T(8,128)(2,1)S(1)} fusion(f32[128,2816]{1,0:T(8,128)S(1)} %fusion.36, bf16[128,2816]{1,0:T(8,128)(2,1)} %collective-permute-done.2, bf16[1,1024,2816]{2,1,0:T(8,128)(2,1)S(1)} %bitcast.110, bf16[128,1024]{1,0:T(8,128)(2,1)S(1)} %bitcast.122, bf16[128,1024]{1,0:T(8,128)(2,1)S(1)} %collective-permute-done, ...), kind=kOutput, calls=%fused_computation.33 | convolution fusion | flops 741212160 | bytes 9175041 | tf_op jit(solution)/shard_map/dot_general | solution.py:170
  92.7 19.1 %collective-permute-done.6 = bf16[192,2816]{1,0:T(8,128)(2,1)S(1)} collective-permute-done((bf16[192,2816]{1,0:T(8,128)(2,1)S(1)}, bf16[192,2816]{1,0:T(8,128)(2,1)S(1)}, u32[]{:S(2)}, u32[]{:S(2)}) %collective-permute-start.6) | collective-permute-done | bytes 1081376 | tf_op jit(solution)/shard_map/ppermute | solution.py:218
  113.1 21.8 %collective-permute-done.7 = bf16[192,2816]{1,0:T(8,128)(2,1)S(1)} collective-permute-done((bf16[192,2816]{1,0:T(8,128)(2,1)S(1)}, bf16[192,2816]{1,0:T(8,128)(2,1)S(1)}, u32[]{:S(2)}, u32[]{:S(2)}) %collective-permute-start.7) | collective-permute-done | bytes 1081376 | tf_op jit(solution)/shard_map/ppermute | solution.py:219
  134.9 1.6 multiply_convert_fusion
  139.1 11.3 %collective-permute-done.3 = bf16[128,2816]{1,0:T(8,128)(2,1)S(1)} collective-permute-done((bf16[128,2816]{1,0:T(8,128)(2,1)S(1)}, bf16[128,2816]{1,0:T(8,128)(2,1)S(1)}, u32[]{:S(2)}, u32[]{:S(2)}) %collective-permute-start.3) | collective-permute-done | bytes 720928 | tf_op jit(solution)/shard_map/ppermute | solution.py:221
  152.7 20.5 %collective-permute-done.8 = bf16[192,2816]{1,0:T(8,128)(2,1)S(1)} collective-permute-done((bf16[192,2816]{1,0:T(8,128)(2,1)S(1)}, bf16[192,2816]{1,0:T(8,128)(2,1)S(1)}, u32[]{:S(2)}, u32[]{:S(2)}) %collective-permute-start.8) | collective-permute-done | bytes 1081376 | tf_op jit(solution)/shard_map/ppermute | solution.py:221
  175.5 3.4 %all-to-all-start.1 = ((bf16[8,16,1024]{2,1,0:T(8,128)(2,1)}), bf16[8,16,1024]{2,1,0:T(8,128)(2,1)S(1)}, u32[]{:S(2)}, u32[]{:S(2)}) async-start(bf16[8,16,1024]{2,1,0:T(8,128)(2,1)} %bitcast.12), calls=%async_computation.1 | async-start | bytes 524288 | tf_op jit(solution)/shard_map/all_to_all | solution.py:183
  180.0 8.7 %all-to-all-done.1 = bf16[8,16,1024]{2,1,0:T(8,128)(2,1)S(1)} async-done(((bf16[8,16,1024]{2,1,0:T(8,128)(2,1)}), bf16[8,16,1024]{2,1,0:T(8,128)(2,1)S(1)}, u32[]{:S(2)}, u32[]{:S(2)}) %all-to-all-start.1) | async-done | bytes 262176 | tf_op jit(solution)/shard_map/all_to_all | solution.py:183
  188.7 3.6 %all-to-all-start.3 = ((bf16[8,24,1024]{2,1,0:T(8,128)(2,1)}), bf16[8,24,1024]{2,1,0:T(8,128)(2,1)S(1)}, u32[]{:S(2)}, u32[]{:S(2)}) async-start(bf16[8,24,1024]{2,1,0:T(8,128)(2,1)} %bitcast.20), calls=%async_computation.3 | async-start | bytes 786432 | tf_op jit(solution)/shard_map/all_to_all | solution.py:183
  192.7 11.4 %all-to-all-done.3 = bf16[8,24,1024]{2,1,0:T(8,128)(2,1)S(1)} async-done(((bf16[8,24,1024]{2,1,0:T(8,128)(2,1)}), bf16[8,24,1024]{2,1,0:T(8,128)(2,1)S(1)}, u32[]{:S(2)}, u32[]{:S(2)}) %all-to-all-start.3) | async-done | bytes 393248 | tf_op jit(solution)/shard_map/all_to_all | solution.py:183
  (79 shorter events, 26.1 us)
Async XLA Ops:
  6.2 2.2 %copy-start = (bf16[1,2048,1024]{2,1,0:T(8,128)(2,1)S(1)}, bf16[1,2048,1024]{2,1,0:T(8,128)(2,1)}, u32[]{:S(2)}) copy-start(bf16[1,2048,1024]{2,1,0:T(8,128)(2,1)} %key_ref.1) | copy-start | bytes 12582916
  8.4 2.2 %copy-start.1 = (bf16[1,2048,1024]{2,1,0:T(8,128)(2,1)S(1)}, bf16[1,2048,1024]{2,1,0:T(8,128)(2,1)}, u32[]{:S(2)}) copy-start(bf16[1,2048,1024]{2,1,0:T(8,128)(2,1)} %value_ref.1) | copy-start | bytes 12582916
  13.4 19.6 %copy-start.6 = (f32[1024]{0:T(1024)S(1)}, f32[1024]{0:T(1024)}, u32[]{:S(2)}) copy-start(f32[1024]{0:T(1024)} %param.22) | copy-start | bytes 12292
  47.8 1.5 collective-permute-start
  48.9 4.3 %copy-start.5 = (bf16[1,1024,2816]{2,1,0:T(8,128)(2,1)S(1)}, bf16[1,1024,2816]{2,1,0:T(8,128)(2,1)}, u32[]{:S(2)}) copy-start(bf16[1,1024,2816]{2,1,0:T(8,128)(2,1)} %param.26) | copy-start | bytes 17301508
  54.1 19.1 %collective-permute-start.1 = (bf16[128,2816]{1,0:T(8,128)(2,1)S(1)}, bf16[128,2816]{1,0:T(8,128)(2,1)}, u32[]{:S(2)}, u32[]{:S(2)}) collective-permute-start(bf16[128,2816]{1,0:T(8,128)(2,1)S(1)} %fusion.42), channel_id=1, source_target_pairs={{0,1},{1,0},{2,3},{3,2},{4,5},{5,4},{6,7},{7,6},{8,9},{9,8},{10,11... | collective-permute-start | bytes 2162696 | tf_op jit(solution)/shard_map/ppermute | solution.py:218
  55.7 15.7 %all-to-all-start.2 = ((bf16[8,24,1024]{2,1,0:T(8,128)(2,1)}), bf16[8,24,1024]{2,1,0:T(8,128)(2,1)S(1)}, u32[]{:S(2)}, u32[]{:S(2)}) async-start(bf16[8,24,1024]{2,1,0:T(8,128)(2,1)} %bitcast.18), calls=%async_computation.2 | async-start | bytes 786432 | tf_op jit(solution)/shard_map/all_to_all | solution.py:183
  59.4 29.3 %collective-permute-start.2 = (bf16[128,2816]{1,0:T(8,128)(2,1)S(1)}, bf16[128,2816]{1,0:T(8,128)(2,1)}, u32[]{:S(2)}, u32[]{:S(2)}) collective-permute-start(bf16[128,2816]{1,0:T(8,128)(2,1)S(1)} %fusion.45), channel_id=1, source_target_pairs={{0,1},{1,0},{2,3},{3,2},{4,5},{5,4},{6,7},{7,6},{8,9},{9,8},{10,11... | collective-permute-start | bytes 2162696 | tf_op jit(solution)/shard_map/ppermute | solution.py:219
  71.5 5.7 %slice-start = ((s8[5767168]{0:T(1024)(128)(4,1)}), s8[4194304]{0:T(1024)(128)(4,1)S(1)}, s32[]{:S(2)}) async-start(s8[5767168]{0:T(1024)(128)(4,1)} %bitcast.107), calls=%async_computation.4 | async-start | bytes 8388608
  71.5 5.7 %slice-start.1 = ((s8[5767168]{0:T(1024)(128)(4,1)}), s8[1572864]{0:T(1024)(128)(4,1)S(1)}, s32[]{:S(2)}) async-start(s8[5767168]{0:T(1024)(128)(4,1)} %bitcast.107), calls=%async_computation.5 | async-start | bytes 3145728
  71.5 5.7 %collective-permute-start.5 = (bf16[192,1024]{1,0:T(8,128)(2,1)S(1)}, bf16[192,1024]{1,0:T(8,128)(2,1)S(1)}, u32[]{:S(2)}, u32[]{:S(2)}) collective-permute-start(bf16[192,1024]{1,0:T(8,128)(2,1)S(1)} %bitcast.113), channel_id=1, source_target_pairs={{0,2},{2,0},{4,6},{6,4},{8,10},{10,8},{12,14},{14,12},{16,18},{18,... | collective-permute-start | bytes 1179656 | tf_op jit(solution)/shard_map/ppermute | solution.py:209
  73.2 15.5 %slice-start.2 = ((s8[5767168]{0:T(1024)(128)(4,1)}), s8[4194304]{0:T(1024)(128)(4,1)S(1)}, s32[]{:S(2)}) async-start(s8[5767168]{0:T(1024)(128)(4,1)} %bitcast.109), calls=%async_computation.6 | async-start | bytes 8388608
  77.1 11.6 %slice-start.3 = ((s8[5767168]{0:T(1024)(128)(4,1)}), s8[1572864]{0:T(1024)(128)(4,1)S(1)}, s32[]{:S(2)}) async-start(s8[5767168]{0:T(1024)(128)(4,1)} %bitcast.109), calls=%async_computation.7 | async-start | bytes 3145728
  78.5 33.2 %collective-permute-start.6 = (bf16[192,2816]{1,0:T(8,128)(2,1)S(1)}, bf16[192,2816]{1,0:T(8,128)(2,1)S(1)}, u32[]{:S(2)}, u32[]{:S(2)}) collective-permute-start(bf16[192,2816]{1,0:T(8,128)(2,1)S(1)} %fusion.30), channel_id=1, source_target_pairs={{0,1},{1,0},{2,3},{3,2},{4,5},{5,4},{6,7},{7,6},{8,9},{9,8},{10,11... | collective-permute-start | bytes 3244040 | tf_op jit(solution)/shard_map/ppermute | solution.py:218
  84.1 50.9 %collective-permute-start.7 = (bf16[192,2816]{1,0:T(8,128)(2,1)S(1)}, bf16[192,2816]{1,0:T(8,128)(2,1)S(1)}, u32[]{:S(2)}, u32[]{:S(2)}) collective-permute-start(bf16[192,2816]{1,0:T(8,128)(2,1)S(1)} %fusion.33), channel_id=1, source_target_pairs={{0,1},{1,0},{2,3},{3,2},{4,5},{5,4},{6,7},{7,6},{8,9},{9,8},{10,11... | collective-permute-start | bytes 3244040 | tf_op jit(solution)/shard_map/ppermute | solution.py:219
  91.1 59.3 %collective-permute-start.3 = (bf16[128,2816]{1,0:T(8,128)(2,1)S(1)}, bf16[128,2816]{1,0:T(8,128)(2,1)S(1)}, u32[]{:S(2)}, u32[]{:S(2)}) collective-permute-start(bf16[128,2816]{1,0:T(8,128)(2,1)S(1)} %multiply_convert_fusion.1), channel_id=1, source_target_pairs={{0,1},{1,0},{2,3},{3,2},{4,5},{5,4},{6,7},{7,6},{8,9},{9,8},{10,11... | collective-permute-start | bytes 2162696 | tf_op jit(solution)/shard_map/ppermute | solution.py:221
  111.8 26.4 %slice-start.4 = ((s8[5767168]{0:T(1024)(128)(4,1)}), s8[4194304]{0:T(1024)(128)(4,1)S(1)}, s32[]{:S(2)}) async-start(s8[5767168]{0:T(1024)(128)(4,1)} %bitcast.111), calls=%async_computation.8 | async-start | bytes 8388608
  113.1 25.0 %slice-start.5 = ((s8[5767168]{0:T(1024)(128)(4,1)}), s8[1572864]{0:T(1024)(128)(4,1)S(1)}, s32[]{:S(2)}) async-start(s8[5767168]{0:T(1024)(128)(4,1)} %bitcast.111), calls=%async_computation.9 | async-start | bytes 3145728
  136.5 36.6 %collective-permute-start.8 = (bf16[192,2816]{1,0:T(8,128)(2,1)S(1)}, bf16[192,2816]{1,0:T(8,128)(2,1)S(1)}, u32[]{:S(2)}, u32[]{:S(2)}) collective-permute-start(bf16[192,2816]{1,0:T(8,128)(2,1)S(1)} %multiply_convert_fusion), channel_id=1, source_target_pairs={{0,1},{1,0},{2,3},{3,2},{4,5},{5,4},{6,7},{7,6},{8,9},{9,8},{10,11... | collective-permute-start | bytes 3244040 | tf_op jit(solution)/shard_map/ppermute | solution.py:221
  151.3 23.3 %collective-permute-start.4 = (bf16[128,1024]{1,0:T(8,128)(2,1)S(1)}, bf16[128,1024]{1,0:T(8,128)(2,1)S(1)}, u32[]{:S(2)}, u32[]{:S(2)}) collective-permute-start(bf16[128,1024]{1,0:T(8,128)(2,1)S(1)} %get-tuple-element.18), channel_id=1, source_target_pairs={{0,2},{2,0},{4,6},{6,4},{8,10},{10,8},{12,14},{14,12},{16,18},{18,... | collective-permute-start | bytes 786440 | tf_op jit(solution)/shard_map/ppermute | solution.py:226
  174.6 17.7 %copy-start.7 = (f32[128,2]{0,1:T(2,128)S(1)}, f32[128,2]{0,1:T(2,128)}, u32[]{:S(2)}) copy-start(f32[128,2]{0,1:T(2,128)} %param.24) | copy-start | bytes 3076
  174.6 4.5 %collective-permute-start.9 = (bf16[192,1024]{1,0:T(8,128)(2,1)S(1)}, bf16[192,1024]{1,0:T(8,128)(2,1)S(1)}, u32[]{:S(2)}, u32[]{:S(2)}) collective-permute-start(bf16[192,1024]{1,0:T(8,128)(2,1)S(1)} %get-tuple-element.20), channel_id=1, source_target_pairs={{0,2},{2,0},{4,6},{6,4},{8,10},{10,8},{12,14},{14,12},{16,18},{18,... | collective-permute-start | bytes 1179656 | tf_op jit(solution)/shard_map/ppermute | solution.py:226
  175.5 13.2 %all-to-all-start.1 = ((bf16[8,16,1024]{2,1,0:T(8,128)(2,1)}), bf16[8,16,1024]{2,1,0:T(8,128)(2,1)S(1)}, u32[]{:S(2)}, u32[]{:S(2)}) async-start(bf16[8,16,1024]{2,1,0:T(8,128)(2,1)} %bitcast.12), calls=%async_computation.1 | async-start | bytes 524288 | tf_op jit(solution)/shard_map/all_to_all | solution.py:183
  188.7 15.5 %all-to-all-start.3 = ((bf16[8,24,1024]{2,1,0:T(8,128)(2,1)}), bf16[8,24,1024]{2,1,0:T(8,128)(2,1)S(1)}, u32[]{:S(2)}, u32[]{:S(2)}) async-start(bf16[8,24,1024]{2,1,0:T(8,128)(2,1)} %bitcast.20), calls=%async_computation.3 | async-start | bytes 786432 | tf_op jit(solution)/shard_map/all_to_all | solution.py:183
  (3 other events, 2.9 us)

commit v2 on v1

--- a/solution.py
+++ b/solution.py
@@ -96,7 +96,7 @@
             jax.ShapeDtypeStruct((row_count, width), jnp.float32),
             jax.ShapeDtypeStruct((row_count, HD), jnp.float32),
         ],
-        compiler_params=pltpu.CompilerParams(vmem_limit_bytes=40 * 1024 * 1024),
+        compiler_params=pltpu.CompilerParams(vmem_limit_bytes=60 * 1024 * 1024),
         cost_estimate=pl.CostEstimate(
             flops=4 * score_count * HD,
             bytes_accessed=4 * cache * width,
@@ -191,6 +191,11 @@
         return (
             jnp.arange(EXPERTS * count, dtype=jnp.int32)[None, :, None] == dest[:, None, :]
         ).astype(jnp.bfloat16)
+
+    def mix_in(mix, onehot, returned):
+        for k in range(2):
+            mix = mix + dot32(onehot[:, :, k], returned) * expert_gates[:, k : k + 1]
+        return mix
 
     mix = 0.0
     before = None
@@ -214,11 +219,15 @@
             dot32(send, w_up).astype(jnp.bfloat16),
         ]
         stages.append((onehot, keep, before))
+    returned = None
     for onehot, keep, sent in stages:
         gate_act = dot32(keep, w_gate) + lax.ppermute(sent[0], "group", swap_group)
         up_act = dot32(keep, w_up) + lax.ppermute(sent[1], "group", swap_group)
         hidden_keep = (jax.nn.silu(gate_act) * up_act).astype(jnp.bfloat16)
         hidden_send = lax.ppermute(hidden_keep, "group", swap_group)
+        if returned is not None:
+            hidden_send, returned = lax.optimization_barrier((hidden_send, returned))
+            mix = mix_in(mix, stages[0][0], returned)
         part_keep = dot32(hidden_keep, w_down).astype(jnp.bfloat16)
         part_send = dot32(hidden_send, w_down).astype(jnp.bfloat16)
         part_own = jnp.where(first_group, part_keep, part_send)
@@ -227,9 +236,7 @@
             part_other, "dp", swap_owner
         ).astype(jnp.float32)
         returned = exchange(summed.astype(jnp.bfloat16))
-        for k in range(2):
-            mix = mix + dot32(onehot[:, :, k], returned) * expert_gates[:, k : k + 1]
-    return mix
+    return mix_in(mix, stages[-1][0], returned)
 
 
 def on_device(
@@ -252,7 +259,11 @@
     attended, mixed_in, squares = attend_local(
         queries, new_keys, new_values, cache_keys, cache_values, lengths, att_gates, resid
     )
-    squares = lax.psum(jnp.sum(squares, axis=1), "group")
+    squares = jnp.sum(squares, axis=1)
+    if lax.axis_size("group") == 2:
+        squares = squares + lax.ppermute(squares, "group", [(0, 1), (1, 0)])
+    else:
+        squares = lax.psum(squares, "group")
     normed = (mixed_in / jnp.sqrt(squares[:, None] / D + 1e-05) * norm_gain[None, :]).astype(
         jnp.bfloat16
     )

time: 206 us -> 192 us (0.932)
  waiting for transfers between devices: 111 us -> 97.4 us
  matrix products: 26.7 us -> 35.2 us
  local copies, waits for them, and re-layouts: 10.7 us -> 4.29 us
  blocking collectives: 20.2 us -> 14.4 us
  starting transfers between devices: 18.2 us -> 20.8 us
    ppermute x2, waiting for transfers between devices: 20.9 us -> 44.2 us  [experts_paired(): gate_act = dot32(keep, w_gate) + lax.ppermute(sent[0], 'group', swap_group)]
    ppermute x2, waiting for transfers between devices: 25.9 us -> 3.98 us  [experts_paired(): up_act = dot32(keep, w_up) + lax.ppermute(sent[1], 'group', swap_group)]
    ppermute x2, waiting for transfers between devices: 31.8 us -> 17.4 us  [experts_paired(): hidden_send = lax.ppermute(hidden_keep, 'group', swap_group)]
    dot_general x16, matrix products: 25.4 us -> 33.9 us  [dot32(): return jnp.dot(left, right, preferred_element_type=jnp.float32)]
    unnamed x29 -> x21, local copies, waits for them, and re-layouts: 8.07 us -> 0.17 us
    psum x1 -> x0, blocking collectives: 5.87 us -> none  [on_device(): squares = lax.psum(jnp.sum(squares, axis=1), 'group')]
    all_to_all x3, waiting for transfers between devices: 31.6 us -> 28.3 us  [exchange(): lax.all_to_all(rows.reshape(EXPERTS, -1, width), 'dp', split_axis=0, conc...]
    ppermute x2, waiting for transfers between devices: 0.01 us -> 3.12 us  [experts_paired(): lax.ppermute(part_other, 'dp', swap_owner).astype(jnp.float32)]
  transfers between devices with their start and end apart: 13 -> 14, of which waited for: 10 -> 11; matrix products, arithmetic and copies ran while one was open for 11% -> 13% of each run, Pallas kernels for 0% -> 0%
where the time goes in v2:
time: 192 us; the launch traced here: 191 us
  waiting for transfers between devices  97.4 us (51%)
  matrix products  35.2 us (18%)
  starting transfers between devices  20.8 us (11%)
  blocking collectives  14.4 us (8%)
  Pallas kernels  12.5 us (7%)
  other arithmetic  4.92 us (3%)
  local copies, waits for them, and re-layouts  4.29 us (2%)
    ppermute x2, waiting for transfers between devices, experts_paired(): gate_act = dot32(keep, w_gate) + lax.ppermute(sent[0], 'group', swap_group)  44.2 us
    dot_general x16, matrix products, dot32(): return jnp.dot(left, right, preferred_element_type=jnp.float32)  33.9 us
    all_to_all x3, waiting for transfers between devices, exchange(): lax.all_to_all(rows.reshape(EXPERTS, -1, width), 'dp', split_axis=0, conc...  28.3 us
    ppermute x2, waiting for transfers between devices, experts_paired(): hidden_send = lax.ppermute(hidden_keep, 'group', swap_group)  17.4 us
    all_to_all x1, blocking collectives, exchange(): lax.all_to_all(rows.reshape(EXPERTS, -1, width), 'dp', split_axis=0, conc...  14.4 us
    pallas_call x1, Pallas kernels, attend_local(): pl.pallas_call(attend_kernel, grid=(heads,), in_specs=[pl.BlockSpec(memor...  12.5 us
    all_to_all x3, starting transfers between devices, exchange(): lax.all_to_all(rows.reshape(EXPERTS, -1, width), 'dp', split_axis=0, conc...  10.8 us
    ppermute x2, waiting for transfers between devices, experts_paired(): up_act = dot32(keep, w_up) + lax.ppermute(sent[1], 'group', swap_group)  3.98 us
  transfers between devices with their start and end apart: 14, of which 11 were waited for; matrix products, arithmetic and copies ran while one was open for 13% of the time, Pallas kernels for 0%

profile of v2, /device:TPU:0, one launch (start us, length us, event | category | flops | bytes accessed | tf_op | source)
XLA Modules:
  0.0 191.1 jit_solution(17228035166291884289)
XLA Ops:
  0.6 2.0 %copy.39 = bf16[2,128,1024]{2,1,0:T(8,128)(2,1)} copy(bf16[2,128,1024]{2,0,1:T(2,128)(2,1)} %bitcast.128) | data formatting | bytes 1048576 | tf_op jit(solution)/shard_map/transpose | solution.py:75
  4.7 12.5 %shard_map.149 = (bf16[128,1024]{1,0:T(8,128)(2,1)}, f32[128,1024]{1,0:T(8,128)}, f32[128,128]{1,0:T(8,128)}) custom-call(s32[1]{0:T(128)S(6)} %copy.51.len_ref, bf16[256,1024]{1,0:T(8,128)(2,1)} %bitcast.126, bf16[128,1024]{1,0:T(8,128)(2,1)} %key_new_ref.1, bf16[128,1024]{1,0:T(8,128)(2,1)} %value_new_ref.1, bf16[1,2048,1024]{2,1,0:T(8,128)(2,1)} %key_ref.1, ...), custom_call_target="tpu_custom_call" | custom-call | flops 2281701376 | bytes 8388608 | tf_op jit(solution)/shard_map/pallas_call | solution.py:80
  18.2 3.0 %collective-permute-start = (f32[128]{0:T(128)S(1)}, f32[128]{0:T(128)S(1)}, u32[]{:S(2)}, u32[]{:S(2)}) collective-permute-start(f32[128]{0:T(128)S(1)} %reduce_sum.44), channel_id=1, source_target_pairs={{0,1},{1,0},{2,3},{3,2},{4,5},{5,4},{6,7},{7,6},{8,9},{9,8},{10,11... | collective-permute-start | bytes 1544 | tf_op jit(solution)/shard_map/ppermute | solution.py:264
  24.4 14.4 %all_to_all.20 = bf16[8,16,1024]{2,1,0:T(8,128)(2,1)S(1)} all-to-all(bf16[8,16,1024]{2,1,0:T(8,128)(2,1)S(1)} %bitcast.127), channel_id=1, replica_groups={{0,4,8,12,16,20,24,28},{2,6,10,14,18,22,26,30},{1,5,9,13,17,21,25,29},{..., dimensions={0} | all-to-all | bytes 524288 | tf_op jit(solution)/shard_map/all_to_all | solution.py:183
  40.3 3.6 %fusion.45 = bf16[128,2816]{1,0:T(8,128)(2,1)S(1)} fusion(bf16[1,1024,2816]{2,1,0:T(8,128)(2,1)} %param.26, bf16[128,1024]{1,0:T(8,128)(2,1)S(1)} %collective-permute-done.1, bf16[128,1024]{1,0:T(8,128)(2,1)S(1)} %bitcast.118, pred[]{:T(512)S(6)} %eq.65), kind=kOutput, calls=%fused_computation.31 | convolution fusion | flops 738689024 | bytes 7012353 | tf_op jit(solution)/shard_map/dot_general | solution.py:170
  43.9 4.4 %fusion.42 = bf16[128,2816]{1,0:T(8,128)(2,1)} fusion(bf16[1,1024,2816]{2,1,0:T(8,128)(2,1)} %param.25, bf16[128,1024]{1,0:T(8,128)(2,1)S(1)} %collective-permute-done.1, bf16[128,1024]{1,0:T(8,128)(2,1)S(1)} %bitcast.119, pred[]{:T(512)S(6)} %eq.65), kind=kOutput, calls=%fused_computation.30 | convolution fusion | flops 738689024 | bytes 7012353 | tf_op jit(solution)/shard_map/dot_general | solution.py:170
  49.6 3.8 %all-to-all-start.1 = ((bf16[8,24,1024]{2,1,0:T(8,128)(2,1)}), bf16[8,24,1024]{2,1,0:T(8,128)(2,1)S(1)}, u32[]{:S(2)}, u32[]{:S(2)}) async-start(bf16[8,24,1024]{2,1,0:T(8,128)(2,1)} %bitcast.11), calls=%async_computation.1 | async-start | bytes 786432 | tf_op jit(solution)/shard_map/all_to_all | solution.py:183
  54.2 10.9 %all-to-all-done.1 = bf16[8,24,1024]{2,1,0:T(8,128)(2,1)S(1)} async-done(((bf16[8,24,1024]{2,1,0:T(8,128)(2,1)}), bf16[8,24,1024]{2,1,0:T(8,128)(2,1)S(1)}, u32[]{:S(2)}, u32[]{:S(2)}) %all-to-all-start.1) | async-done | bytes 393248 | tf_op jit(solution)/shard_map/all_to_all | solution.py:183
  65.1 2.6 %collective-permute-done.6 = bf16[128,2816]{1,0:T(8,128)(2,1)} collective-permute-done((bf16[128,2816]{1,0:T(8,128)(2,1)}, bf16[128,2816]{1,0:T(8,128)(2,1)}, u32[]{:S(2)}, u32[]{:S(2)}) %collective-permute-start.6) | collective-permute-done | bytes 720928 | tf_op jit(solution)/shard_map/ppermute | solution.py:224
  67.7 3.9 %fusion.36 = f32[128,2816]{1,0:T(8,128)S(1)} fusion(bf16[1,1024,2816]{2,1,0:T(8,128)(2,1)} %param.25, bf16[128,2816]{1,0:T(8,128)(2,1)} %collective-permute-done.6, bf16[128,1024]{1,0:T(8,128)(2,1)S(1)} %bitcast.120, bf16[128,1024]{1,0:T(8,128)(2,1)S(1)} %collective-permute-done.1, pred[]{:T(512)S(6)} %eq.65), kind=kOutput, calls=%fused_computation.28 | convolution fusion | flops 739049472 | bytes 8454145 | tf_op jit(solution)/shard_map/dot_general | solution.py:170
  71.6 4.1 %fusion.33 = bf16[192,2816]{1,0:T(8,128)(2,1)S(1)} fusion(bf16[1,1024,2816]{2,1,0:T(8,128)(2,1)} %param.26, bf16[192,1024]{1,0:T(8,128)(2,1)S(1)} %collective-permute-done.2, bf16[192,1024]{1,0:T(8,128)(2,1)S(1)} %bitcast.113, pred[]{:T(512)S(6)} %eq.65), kind=kOutput, calls=%fused_computation.27 | convolution fusion | flops 1108033536 | bytes 7634945 | tf_op jit(solution)/shard_map/dot_general | solution.py:170
  79.1 4.0 %collective-permute-done.7 = bf16[128,2816]{1,0:T(8,128)(2,1)} collective-permute-done((bf16[128,2816]{1,0:T(8,128)(2,1)S(1)}, bf16[128,2816]{1,0:T(8,128)(2,1)}, u32[]{:S(2)}, u32[]{:S(2)}) %collective-permute-start.7) | collective-permute-done | bytes 720928 | tf_op jit(solution)/shard_map/ppermute | solution.py:225
  83.1 2.4 %multiply_convert_fusion.1 = bf16[128,2816]{1,0:T(8,128)(2,1)S(1)} fusion(f32[128,2816]{1,0:T(8,128)S(1)} %fusion.36, bf16[128,2816]{1,0:T(8,128)(2,1)} %collective-permute-done.7, bf16[1,1024,2816]{2,1,0:T(8,128)(2,1)S(1)} %bitcast.109, bf16[128,1024]{1,0:T(8,128)(2,1)S(1)} %bitcast.121, bf16[128,1024]{1,0:T(8,128)(2,1)S(1)} %collective-permute-done.1, ...), kind=kOutput, calls=%fused_computation.33 | convolution fusion | flops 741212160 | bytes 9175041 | tf_op jit(solution)/shard_map/dot_general | solution.py:170
  87.7 41.6 %collective-permute-done.3 = bf16[192,2816]{1,0:T(8,128)(2,1)S(1)} collective-permute-done((bf16[192,2816]{1,0:T(8,128)(2,1)S(1)}, bf16[192,2816]{1,0:T(8,128)(2,1)S(1)}, u32[]{:S(2)}, u32[]{:S(2)}) %collective-permute-start.3) | collective-permute-done | bytes 1081376 | tf_op jit(solution)/shard_map/ppermute | solution.py:224
  130.7 1.5 multiply_convert_fusion
  133.6 11.2 %collective-permute-done.8 = bf16[128,2816]{1,0:T(8,128)(2,1)S(1)} collective-permute-done((bf16[128,2816]{1,0:T(8,128)(2,1)S(1)}, bf16[128,2816]{1,0:T(8,128)(2,1)S(1)}, u32[]{:S(2)}, u32[]{:S(2)}) %collective-permute-start.8) | collective-permute-done | bytes 720928 | tf_op jit(solution)/shard_map/ppermute | solution.py:227
  148.1 3.4 %all-to-all-start.2 = ((bf16[8,16,1024]{2,1,0:T(8,128)(2,1)}), bf16[8,16,1024]{2,1,0:T(8,128)(2,1)S(1)}, u32[]{:S(2)}, u32[]{:S(2)}) async-start(bf16[8,16,1024]{2,1,0:T(8,128)(2,1)} %bitcast.14), calls=%async_computation.2 | async-start | bytes 524288 | tf_op jit(solution)/shard_map/all_to_all | solution.py:183
  151.6 3.9 %fusion.48 = bf16[192,1024]{1,0:T(8,128)(2,1)S(1)} fusion(bf16[192,2816]{1,0:T(8,128)(2,1)S(1)} %multiply_convert_fusion, bf16[1,2816,1024]{2,1,0:T(8,128)(2,1)} %param.27), kind=kOutput, calls=%fused_computation.34 | convolution fusion | flops 1107492864 | bytes 7241728 | tf_op jit(solution)/shard_map/dot_general | solution.py:170
  155.5 5.5 %all-to-all-done.2 = bf16[8,16,1024]{2,1,0:T(8,128)(2,1)S(1)} async-done(((bf16[8,16,1024]{2,1,0:T(8,128)(2,1)}), bf16[8,16,1024]{2,1,0:T(8,128)(2,1)S(1)}, u32[]{:S(2)}, u32[]{:S(2)}) %all-to-all-start.2) | async-done | bytes 262176 | tf_op jit(solution)/shard_map/all_to_all | solution.py:183
  161.0 6.2 %collective-permute-done.5 = bf16[192,2816]{1,0:T(8,128)(2,1)S(1)} collective-permute-done((bf16[192,2816]{1,0:T(8,128)(2,1)S(1)}, bf16[192,2816]{1,0:T(8,128)(2,1)S(1)}, u32[]{:S(2)}, u32[]{:S(2)}) %collective-permute-start.5) | collective-permute-done | bytes 1081376 | tf_op jit(solution)/shard_map/ppermute | solution.py:227
  167.2 3.9 %broadcast_select_fusion = (bf16[192,1024]{1,0:T(8,128)(2,1)S(1)}, bf16[192,1024]{1,0:T(8,128)(2,1)S(1)}) fusion(bf16[192,1024]{1,0:T(8,128)(2,1)S(1)} %fusion.48, pred[]{:T(512)S(6)} %eq.65, bf16[192,2816]{1,0:T(8,128)(2,1)S(1)} %collective-permute-done.5, bf16[1,2816,1024]{2,1,0:T(8,128)(2,1)} %param.27), kind=kOutput, calls=%fused_computation.52 | convolution fusion | flops 1107689472 | bytes 8028161 | tf_op jit(solution)/shard_map/dot_general | solution.py:170
  171.3 1.6 collective-permute-done.10
  173.8 3.6 %all-to-all-start.3 = ((bf16[8,24,1024]{2,1,0:T(8,128)(2,1)}), bf16[8,24,1024]{2,1,0:T(8,128)(2,1)S(1)}, u32[]{:S(2)}, u32[]{:S(2)}) async-start(bf16[8,24,1024]{2,1,0:T(8,128)(2,1)} %bitcast.20), calls=%async_computation.3 | async-start | bytes 786432 | tf_op jit(solution)/shard_map/all_to_all | solution.py:183
  177.7 11.9 %all-to-all-done.3 = bf16[8,24,1024]{2,1,0:T(8,128)(2,1)S(1)} async-done(((bf16[8,24,1024]{2,1,0:T(8,128)(2,1)}), bf16[8,24,1024]{2,1,0:T(8,128)(2,1)S(1)}, u32[]{:S(2)}, u32[]{:S(2)}) %all-to-all-start.3) | async-done | bytes 393248 | tf_op jit(solution)/shard_map/all_to_all | solution.py:183
  (72 shorter events, 23.8 us)
Async XLA Ops:
  4.7 16.5 %copy-start.2 = (s32[128,2]{0,1:T(2,128)S(1)}, s32[128,2]{0,1:T(2,128)}, u32[]{:S(2)}) copy-start(s32[128,2]{0,1:T(2,128)} %param.23) | copy-start | bytes 3076
  4.7 18.3 %copy-start.1 = (f32[1024]{0:T(1024)S(1)}, f32[1024]{0:T(1024)}, u32[]{:S(2)}) copy-start(f32[1024]{0:T(1024)} %param.22) | copy-start | bytes 12292
  18.2 4.7 %collective-permute-start = (f32[128]{0:T(128)S(1)}, f32[128]{0:T(128)S(1)}, u32[]{:S(2)}, u32[]{:S(2)}) collective-permute-start(f32[128]{0:T(128)S(1)} %reduce_sum.44), channel_id=1, source_target_pairs={{0,1},{1,0},{2,3},{3,2},{4,5},{5,4},{6,7},{7,6},{8,9},{9,8},{10,11... | collective-permute-start | bytes 1544 | tf_op jit(solution)/shard_map/ppermute | solution.py:264
  38.8 1.5 collective-permute-start.1
  48.3 19.3 %collective-permute-start.6 = (bf16[128,2816]{1,0:T(8,128)(2,1)}, bf16[128,2816]{1,0:T(8,128)(2,1)}, u32[]{:S(2)}, u32[]{:S(2)}) collective-permute-start(bf16[128,2816]{1,0:T(8,128)(2,1)} %fusion.42), channel_id=1, source_target_pairs={{0,1},{1,0},{2,3},{3,2},{4,5},{5,4},{6,7},{7,6},{8,9},{9,8},{10,11... | collective-permute-start | bytes 2162696 | tf_op jit(solution)/shard_map/ppermute | solution.py:224
  49.6 27.4 %slice-start = ((s8[5767168]{0:T(1024)(128)(4,1)}), s8[1572864]{0:T(1024)(128)(4,1)S(1)}, s32[]{:S(2)}) async-start(s8[5767168]{0:T(1024)(128)(4,1)} %bitcast.106), calls=%async_computation.4 | async-start | bytes 3145728
  49.6 15.5 %all-to-all-start.1 = ((bf16[8,24,1024]{2,1,0:T(8,128)(2,1)}), bf16[8,24,1024]{2,1,0:T(8,128)(2,1)S(1)}, u32[]{:S(2)}, u32[]{:S(2)}) async-start(bf16[8,24,1024]{2,1,0:T(8,128)(2,1)} %bitcast.11), calls=%async_computation.1 | async-start | bytes 786432 | tf_op jit(solution)/shard_map/all_to_all | solution.py:183
  53.4 29.7 %collective-permute-start.7 = (bf16[128,2816]{1,0:T(8,128)(2,1)S(1)}, bf16[128,2816]{1,0:T(8,128)(2,1)}, u32[]{:S(2)}, u32[]{:S(2)}) collective-permute-start(bf16[128,2816]{1,0:T(8,128)(2,1)S(1)} %fusion.45), channel_id=1, source_target_pairs={{0,1},{1,0},{2,3},{3,2},{4,5},{5,4},{6,7},{7,6},{8,9},{9,8},{10,11... | collective-permute-start | bytes 2162696 | tf_op jit(solution)/shard_map/ppermute | solution.py:225
  65.1 11.9 %slice-start.1 = ((s8[5767168]{0:T(1024)(128)(4,1)}), s8[4194304]{0:T(1024)(128)(4,1)S(1)}, s32[]{:S(2)}) async-start(s8[5767168]{0:T(1024)(128)(4,1)} %bitcast.106), calls=%async_computation.5 | async-start | bytes 8388608
  65.1 6.5 %collective-permute-start.2 = (bf16[192,1024]{1,0:T(8,128)(2,1)S(1)}, bf16[192,1024]{1,0:T(8,128)(2,1)S(1)}, u32[]{:S(2)}, u32[]{:S(2)}) collective-permute-start(bf16[192,1024]{1,0:T(8,128)(2,1)S(1)} %bitcast.112), channel_id=1, source_target_pairs={{0,2},{2,0},{4,6},{6,4},{8,10},{10,8},{12,14},{14,12},{16,18},{18,... | collective-permute-start | bytes 1179656 | tf_op jit(solution)/shard_map/ppermute | solution.py:214
  67.6 15.5 %slice-start.2 = ((s8[5767168]{0:T(1024)(128)(4,1)}), s8[4194304]{0:T(1024)(128)(4,1)S(1)}, s32[]{:S(2)}) async-start(s8[5767168]{0:T(1024)(128)(4,1)} %bitcast.108), calls=%async_computation.6 | async-start | bytes 8388608
  71.5 11.6 %slice-start.3 = ((s8[5767168]{0:T(1024)(128)(4,1)}), s8[1572864]{0:T(1024)(128)(4,1)S(1)}, s32[]{:S(2)}) async-start(s8[5767168]{0:T(1024)(128)(4,1)} %bitcast.108), calls=%async_computation.7 | async-start | bytes 3145728
  75.6 55.1 %collective-permute-start.4 = (bf16[192,2816]{1,0:T(8,128)(2,1)S(1)}, bf16[192,2816]{1,0:T(8,128)(2,1)S(1)}, u32[]{:S(2)}, u32[]{:S(2)}) collective-permute-start(bf16[192,2816]{1,0:T(8,128)(2,1)S(1)} %fusion.33), channel_id=1, source_target_pairs={{0,1},{1,0},{2,3},{3,2},{4,5},{5,4},{6,7},{7,6},{8,9},{9,8},{10,11... | collective-permute-start | bytes 3244040 | tf_op jit(solution)/shard_map/ppermute | solution.py:225
  77.0 9.8 %slice-start.4 = ((s8[5767168]{0:T(1024)(128)(4,1)}), s8[4194304]{0:T(1024)(128)(4,1)S(1)}, s32[]{:S(2)}) async-start(s8[5767168]{0:T(1024)(128)(4,1)} %bitcast.110), calls=%async_computation.8 | async-start | bytes 8388608
  78.3 8.5 %slice-start.5 = ((s8[5767168]{0:T(1024)(128)(4,1)}), s8[1572864]{0:T(1024)(128)(4,1)S(1)}, s32[]{:S(2)}) async-start(s8[5767168]{0:T(1024)(128)(4,1)} %bitcast.110), calls=%async_computation.9 | async-start | bytes 3145728
  78.3 51.0 %collective-permute-start.3 = (bf16[192,2816]{1,0:T(8,128)(2,1)S(1)}, bf16[192,2816]{1,0:T(8,128)(2,1)S(1)}, u32[]{:S(2)}, u32[]{:S(2)}) collective-permute-start(bf16[192,2816]{1,0:T(8,128)(2,1)S(1)} %fusion.30), channel_id=1, source_target_pairs={{0,1},{1,0},{2,3},{3,2},{4,5},{5,4},{6,7},{7,6},{8,9},{9,8},{10,11... | collective-permute-start | bytes 3244040 | tf_op jit(solution)/shard_map/ppermute | solution.py:224
  85.5 59.3 %collective-permute-start.8 = (bf16[128,2816]{1,0:T(8,128)(2,1)S(1)}, bf16[128,2816]{1,0:T(8,128)(2,1)S(1)}, u32[]{:S(2)}, u32[]{:S(2)}) collective-permute-start(bf16[128,2816]{1,0:T(8,128)(2,1)S(1)} %multiply_convert_fusion.1), channel_id=1, source_target_pairs={{0,1},{1,0},{2,3},{3,2},{4,5},{5,4},{6,7},{7,6},{8,9},{9,8},{10,11... | collective-permute-start | bytes 2162696 | tf_op jit(solution)/shard_map/ppermute | solution.py:227
  132.3 34.9 %collective-permute-start.5 = (bf16[192,2816]{1,0:T(8,128)(2,1)S(1)}, bf16[192,2816]{1,0:T(8,128)(2,1)S(1)}, u32[]{:S(2)}, u32[]{:S(2)}) collective-permute-start(bf16[192,2816]{1,0:T(8,128)(2,1)S(1)} %multiply_convert_fusion), channel_id=1, source_target_pairs={{0,1},{1,0},{2,3},{3,2},{4,5},{5,4},{6,7},{7,6},{8,9},{9,8},{10,11... | collective-permute-start | bytes 3244040 | tf_op jit(solution)/shard_map/ppermute | solution.py:227
  145.7 1.6 collective-permute-start.9
  148.1 12.9 %all-to-all-start.2 = ((bf16[8,16,1024]{2,1,0:T(8,128)(2,1)}), bf16[8,16,1024]{2,1,0:T(8,128)(2,1)S(1)}, u32[]{:S(2)}, u32[]{:S(2)}) async-start(bf16[8,16,1024]{2,1,0:T(8,128)(2,1)} %bitcast.14), calls=%async_computation.2 | async-start | bytes 524288 | tf_op jit(solution)/shard_map/all_to_all | solution.py:183
  171.1 6.3 %copy-start.3 = (f32[128,2]{0,1:T(2,128)S(1)}, f32[128,2]{0,1:T(2,128)}, u32[]{:S(2)}) copy-start(f32[128,2]{0,1:T(2,128)} %param.24) | copy-start | bytes 3076
  171.1 1.8 collective-permute-start.10
  173.8 16.3 %copy-start = (f32[128,1024]{1,0:T(8,128)S(1)}, f32[128,1024]{1,0:T(8,128)}, u32[]{:S(2)}) copy-start(f32[128,1024]{1,0:T(8,128)} %get-tuple-element.11) | copy-start | bytes 1572868
  173.8 15.8 %all-to-all-start.3 = ((bf16[8,24,1024]{2,1,0:T(8,128)(2,1)}), bf16[8,24,1024]{2,1,0:T(8,128)(2,1)S(1)}, u32[]{:S(2)}, u32[]{:S(2)}) async-start(bf16[8,24,1024]{2,1,0:T(8,128)(2,1)} %bitcast.20), calls=%async_computation.3 | async-start | bytes 786432 | tf_op jit(solution)/shard_map/all_to_all | solution.py:183

commit v3 on v2

--- a/solution.py
+++ b/solution.py
@@ -163,7 +163,7 @@
     return jnp.sum(picked * expert_gates[:, :, None], axis=1)
 
 
-CHUNKS = ((0, 16), (16, 24))
+CHUNKS = ((0, 16), (16, 16), (32, 8))
 
 
 def dot32(left, right):
@@ -220,14 +220,14 @@
         ]
         stages.append((onehot, keep, before))
     returned = None
-    for onehot, keep, sent in stages:
+    for index, (_, keep, sent) in enumerate(stages):
         gate_act = dot32(keep, w_gate) + lax.ppermute(sent[0], "group", swap_group)
         up_act = dot32(keep, w_up) + lax.ppermute(sent[1], "group", swap_group)
         hidden_keep = (jax.nn.silu(gate_act) * up_act).astype(jnp.bfloat16)
         hidden_send = lax.ppermute(hidden_keep, "group", swap_group)
         if returned is not None:
             hidden_send, returned = lax.optimization_barrier((hidden_send, returned))
-            mix = mix_in(mix, stages[0][0], returned)
+            mix = mix_in(mix, stages[index - 1][0], returned)
         part_keep = dot32(hidden_keep, w_down).astype(jnp.bfloat16)
         part_send = dot32(hidden_send, w_down).astype(jnp.bfloat16)
         part_own = jnp.where(first_group, part_keep, part_send)

time: 192 us -> 210 us (1.094)
  matrix products: 35.2 us -> 64.8 us
  starting transfers between devices: 20.8 us -> 40.6 us
  waiting for transfers between devices: 97.4 us -> 79.3 us
  blocking collectives: 14.4 us -> 0 us
    dot_general x16 -> x24, matrix products: 33.9 us -> 62 us  [dot32(): return jnp.dot(left, right, preferred_element_type=jnp.float32)]
    ppermute x2 -> x3, waiting for transfers between devices: 44.2 us -> 25.9 us  [experts_paired(): gate_act = dot32(keep, w_gate) + lax.ppermute(sent[0], 'group', swap_group)]
    all_to_all x3 -> x6, starting transfers between devices: 10.8 us -> 27.2 us  [exchange(): lax.all_to_all(rows.reshape(EXPERTS, -1, width), 'dp', split_axis=0, conc...]
    all_to_all x1 -> x0, blocking collectives: 14.4 us -> none  [exchange(): lax.all_to_all(rows.reshape(EXPERTS, -1, width), 'dp', split_axis=0, conc...]
    ppermute x2 -> x3, waiting for transfers between devices: 3.98 us -> 14.5 us  [experts_paired(): up_act = dot32(keep, w_up) + lax.ppermute(sent[1], 'group', swap_group)]
    ppermute x2 -> x3, waiting for transfers between devices: 17.4 us -> 7.66 us  [experts_paired(): hidden_send = lax.ppermute(hidden_keep, 'group', swap_group)]
    all_to_all x3 -> x6, waiting for transfers between devices: 28.3 us -> 29.6 us  [exchange(): lax.all_to_all(rows.reshape(EXPERTS, -1, width), 'dp', split_axis=0, conc...]
  transfers between devices with their start and end apart: 14 -> 22, of which waited for: 11 -> 13; matrix products, arithmetic and copies ran while one was open for 13% -> 26% of each run, Pallas kernels for 0% -> 0%
where the time goes in v3:
time: 210 us; the launch traced here: 209 us
  waiting for transfers between devices  79.3 us (38%)
  matrix products  64.8 us (31%)
  starting transfers between devices  40.6 us (19%)
  Pallas kernels  12.5 us (6%)
  other arithmetic  5.67 us (3%)
  local copies, waits for them, and re-layouts  4.33 us (2%)
    dot_general x24, matrix products, dot32(): return jnp.dot(left, right, preferred_element_type=jnp.float32)  62 us
    all_to_all x6, waiting for transfers between devices, exchange(): lax.all_to_all(rows.reshape(EXPERTS, -1, width), 'dp', split_axis=0, conc...  29.6 us
    all_to_all x6, starting transfers between devices, exchange(): lax.all_to_all(rows.reshape(EXPERTS, -1, width), 'dp', split_axis=0, conc...  27.2 us
    ppermute x3, waiting for transfers between devices, experts_paired(): gate_act = dot32(keep, w_gate) + lax.ppermute(sent[0], 'group', swap_group)  25.9 us
    ppermute x3, waiting for transfers between devices, experts_paired(): up_act = dot32(keep, w_up) + lax.ppermute(sent[1], 'group', swap_group)  14.5 us
    pallas_call x1, Pallas kernels, attend_local(): pl.pallas_call(attend_kernel, grid=(heads,), in_specs=[pl.BlockSpec(memor...  12.5 us
    ppermute x3, waiting for transfers between devices, experts_paired(): hidden_send = lax.ppermute(hidden_keep, 'group', swap_group)  7.66 us
  transfers between devices with their start and end apart: 22, of which 13 were waited for; matrix products, arithmetic and copies ran while one was open for 26% of the time, Pallas kernels for 0%

profile of v3, /device:TPU:0, one launch (start us, length us, event | category | flops | bytes accessed | tf_op | source)
XLA Modules:
  0.0 208.8 jit_solution(7166461401232322458)
XLA Ops:
  4.8 12.5 %shard_map.149 = (bf16[128,1024]{1,0:T(8,128)(2,1)}, f32[128,1024]{1,0:T(8,128)}, f32[128,128]{1,0:T(8,128)}) custom-call(s32[1]{0:T(128)S(6)} %copy.57.len_ref, bf16[256,1024]{1,0:T(8,128)(2,1)} %bitcast.192, bf16[128,1024]{1,0:T(8,128)(2,1)} %key_new_ref.1, bf16[128,1024]{1,0:T(8,128)(2,1)} %value_new_ref.1, bf16[1,2048,1024]{2,1,0:T(8,128)(2,1)} %key_ref.1, ...), custom_call_target="tpu_custom_call" | custom-call | flops 2281701376 | bytes 8388608 | tf_op jit(solution)/shard_map/pallas_call | solution.py:80
  25.1 6.1 %all-to-all-start = ((bf16[8,16,1024]{2,1,0:T(8,128)(2,1)}), bf16[8,16,1024]{2,1,0:T(8,128)(2,1)S(1)}, u32[]{:S(2)}, u32[]{:S(2)}) async-start(bf16[8,16,1024]{2,1,0:T(8,128)(2,1)} %bitcast.7), calls=%async_computation | async-start | bytes 524288 | tf_op jit(solution)/shard_map/all_to_all | solution.py:183
  31.4 8.3 %all-to-all-done = bf16[8,16,1024]{2,1,0:T(8,128)(2,1)S(1)} async-done(((bf16[8,16,1024]{2,1,0:T(8,128)(2,1)}), bf16[8,16,1024]{2,1,0:T(8,128)(2,1)S(1)}, u32[]{:S(2)}, u32[]{:S(2)}) %all-to-all-start) | async-done | bytes 262176 | tf_op jit(solution)/shard_map/all_to_all | solution.py:183
  44.8 4.4 %fusion.48 = bf16[128,2816]{1,0:T(8,128)(2,1)} fusion(bf16[1,1024,2816]{2,1,0:T(8,128)(2,1)} %param.25, bf16[128,1024]{1,0:T(8,128)(2,1)S(1)} %collective-permute-done.1, bf16[128,1024]{1,0:T(8,128)(2,1)S(1)} %bitcast.184, pred[]{:T(512)S(6)} %eq.78), kind=kOutput, calls=%fused_computation.40 | convolution fusion | flops 738689024 | bytes 7012353 | tf_op jit(solution)/shard_map/dot_general | solution.py:170
  55.8 7.5 %all-to-all-done.1 = bf16[8,16,1024]{2,1,0:T(8,128)(2,1)S(1)} async-done(((bf16[8,16,1024]{2,1,0:T(8,128)(2,1)}), bf16[8,16,1024]{2,1,0:T(8,128)(2,1)S(1)}, u32[]{:S(2)}, u32[]{:S(2)}) %all-to-all-start.1) | async-done | bytes 262176 | tf_op jit(solution)/shard_map/all_to_all | solution.py:183
  63.3 5.3 %collective-permute-done.6 = bf16[128,2816]{1,0:T(8,128)(2,1)} collective-permute-done((bf16[128,2816]{1,0:T(8,128)(2,1)}, bf16[128,2816]{1,0:T(8,128)(2,1)}, u32[]{:S(2)}, u32[]{:S(2)}) %collective-permute-start.6) | collective-permute-done | bytes 720928 | tf_op jit(solution)/shard_map/ppermute | solution.py:224
  68.6 4.9 %fusion.39 = f32[128,2816]{1,0:T(8,128)} fusion(bf16[1,1024,2816]{2,1,0:T(8,128)(2,1)} %param.25, bf16[128,2816]{1,0:T(8,128)(2,1)} %collective-permute-done.6, bf16[128,1024]{1,0:T(8,128)(2,1)S(1)} %bitcast.185, bf16[128,1024]{1,0:T(8,128)(2,1)S(1)} %collective-permute-done.1, pred[]{:T(512)S(6)} %eq.78), kind=kOutput, calls=%fused_computation.37 | convolution fusion | flops 739049472 | bytes 8454145 | tf_op jit(solution)/shard_map/dot_general | solution.py:170
  73.4 4.4 %fusion.57 = bf16[128,2816]{1,0:T(8,128)(2,1)} fusion(bf16[1,1024,2816]{2,1,0:T(8,128)(2,1)} %param.26, bf16[128,1024]{1,0:T(8,128)(2,1)S(1)} %collective-permute-done.2, bf16[128,1024]{1,0:T(8,128)(2,1)S(1)} %bitcast.178, pred[]{:T(512)S(6)} %eq.78), kind=kOutput, calls=%fused_computation.43 | convolution fusion | flops 738689024 | bytes 7012353 | tf_op jit(solution)/shard_map/dot_general | solution.py:170
  83.2 4.4 %multiply_convert_fusion = bf16[128,2816]{1,0:T(8,128)(2,1)S(1)} fusion(f32[128,2816]{1,0:T(8,128)} %fusion.39, bf16[128,2816]{1,0:T(8,128)(2,1)} %collective-permute-done.7, bf16[1,1024,2816]{2,1,0:T(8,128)(2,1)} %param.26, bf16[128,1024]{1,0:T(8,128)(2,1)S(1)} %bitcast.186, bf16[128,1024]{1,0:T(8,128)(2,1)S(1)} %collective-permute-done.1, pred[]{:T(512)S(6)} %eq.78), kind=kOutput, calls=%fused_computation.48 | convolution fusion | flops 741212160 | bytes 9175041 | tf_op jit(solution)/shard_map/dot_general | solution.py:170
  90.5 3.7 %fusion.79 = bf16[128,1024]{1,0:T(8,128)(2,1)S(1)} fusion(bf16[128,2816]{1,0:T(8,128)(2,1)S(1)} %multiply_convert_fusion, bf16[1,2816,1024]{2,1,0:T(8,128)(2,1)} %param.27), kind=kOutput, calls=%fused_computation.63 | convolution fusion | flops 738328576 | bytes 6750208 | tf_op jit(solution)/shard_map/dot_general | solution.py:170
  96.3 4.5 %fusion.69 = bf16[64,2816]{1,0:T(8,128)(2,1)} fusion(bf16[1,1024,2816]{2,1,0:T(8,128)(2,1)} %param.26, bf16[64,1024]{1,0:T(8,128)(2,1)S(1)} %collective-permute-done.10, pred[]{:T(512)S(6)} %eq.78, bf16[8,8,1024]{2,1,0:T(8,128)(2,1)S(1)} %all-to-all-done.3), kind=kOutput, calls=%fused_computation.47 | convolution fusion | flops 369344512 | bytes 6389761 | tf_op jit(solution)/shard_map/dot_general | solution.py:170
  107.9 14.3 %collective-permute-done.3 = bf16[128,2816]{1,0:T(8,128)(2,1)S(1)} collective-permute-done((bf16[128,2816]{1,0:T(8,128)(2,1)}, bf16[128,2816]{1,0:T(8,128)(2,1)S(1)}, u32[]{:S(2)}, u32[]{:S(2)}) %collective-permute-start.3) | collective-permute-done | bytes 720928 | tf_op jit(solution)/shard_map/ppermute | solution.py:224
  123.2 14.5 %collective-permute-done.4 = bf16[128,2816]{1,0:T(8,128)(2,1)S(1)} collective-permute-done((bf16[128,2816]{1,0:T(8,128)(2,1)}, bf16[128,2816]{1,0:T(8,128)(2,1)S(1)}, u32[]{:S(2)}, u32[]{:S(2)}) %collective-permute-start.4) | collective-permute-done | bytes 720928 | tf_op jit(solution)/shard_map/ppermute | solution.py:225
  141.1 5.7 %all-to-all-start.2 = ((bf16[8,16,1024]{2,1,0:T(8,128)(2,1)}), bf16[8,16,1024]{2,1,0:T(8,128)(2,1)S(1)}, u32[]{:S(2)}, u32[]{:S(2)}) async-start(bf16[8,16,1024]{2,1,0:T(8,128)(2,1)} %bitcast.14), calls=%async_computation.2 | async-start | bytes 524288 | tf_op jit(solution)/shard_map/all_to_all | solution.py:183
  146.8 6.3 %collective-permute-done.11 = bf16[64,2816]{1,0:T(8,128)(2,1)S(1)} collective-permute-done((bf16[64,2816]{1,0:T(8,128)(2,1)}, bf16[64,2816]{1,0:T(8,128)(2,1)S(1)}, u32[]{:S(2)}, u32[]{:S(2)}) %collective-permute-start.11) | collective-permute-done | bytes 360480 | tf_op jit(solution)/shard_map/ppermute | solution.py:224
  153.1 4.6 %fusion.60 = f32[64,2816]{1,0:T(8,128)} fusion(bf16[1,1024,2816]{2,1,0:T(8,128)(2,1)} %param.25, bf16[64,2816]{1,0:T(8,128)(2,1)S(1)} %collective-permute-done.11, bf16[64,1024]{1,0:T(8,128)(2,1)S(1)} %collective-permute-done.10, pred[]{:T(512)S(6)} %eq.78, bf16[8,8,1024]{2,1,0:T(8,128)(2,1)S(1)} %all-to-all-done.3), kind=kOutput, calls=%fused_computation.44 | convolution fusion | flops 369524736 | bytes 7110657 | tf_op jit(solution)/shard_map/dot_general | solution.py:170
  161.3 5.5 %collective-permute-done.5 = bf16[128,2816]{1,0:T(8,128)(2,1)S(1)} collective-permute-done((bf16[128,2816]{1,0:T(8,128)(2,1)S(1)}, bf16[128,2816]{1,0:T(8,128)(2,1)S(1)}, u32[]{:S(2)}, u32[]{:S(2)}) %collective-permute-start.5) | collective-permute-done | bytes 720928 | tf_op jit(solution)/shard_map/ppermute | solution.py:227
  170.5 3.8 %multiply_convert_fusion.2 = bf16[64,2816]{1,0:T(8,128)(2,1)S(1)} fusion(f32[64,2816]{1,0:T(8,128)S(1)} %copy-done.1, bf16[64,2816]{1,0:T(8,128)(2,1)} %collective-permute-done.12, bf16[1,1024,2816]{2,1,0:T(8,128)(2,1)} %param.26, bf16[64,1024]{1,0:T(8,128)(2,1)S(1)} %collective-permute-done.10, pred[]{:T(512)S(6)} %eq.78, ...), kind=kOutput, calls=%fused_computation.72 | convolution fusion | flops 370606080 | bytes 7471105 | tf_op jit(solution)/shard_map/dot_general | solution.py:170
  176.5 4.7 %all-to-all-start.4 = ((bf16[8,16,1024]{2,1,0:T(8,128)(2,1)}), bf16[8,16,1024]{2,1,0:T(8,128)(2,1)S(1)}, u32[]{:S(2)}, u32[]{:S(2)}) async-start(bf16[8,16,1024]{2,1,0:T(8,128)(2,1)} %bitcast.22), calls=%async_computation.4 | async-start | bytes 524288 | tf_op jit(solution)/shard_map/all_to_all | solution.py:183
  181.2 3.7 %fusion.91 = bf16[64,1024]{1,0:T(8,128)(2,1)S(1)} fusion(bf16[64,2816]{1,0:T(8,128)(2,1)S(1)} %multiply_convert_fusion.2, bf16[1,2816,1024]{2,1,0:T(8,128)(2,1)} %param.27), kind=kOutput, calls=%fused_computation.70 | convolution fusion | flops 369164288 | bytes 6258688 | tf_op jit(solution)/shard_map/dot_general | solution.py:170
  185.2 5.2 %all-to-all-done.4 = bf16[8,16,1024]{2,1,0:T(8,128)(2,1)S(1)} async-done(((bf16[8,16,1024]{2,1,0:T(8,128)(2,1)}), bf16[8,16,1024]{2,1,0:T(8,128)(2,1)S(1)}, u32[]{:S(2)}, u32[]{:S(2)}) %all-to-all-start.4) | async-done | bytes 262176 | tf_op jit(solution)/shard_map/all_to_all | solution.py:183
  190.4 3.7 %broadcast_select_fusion.6 = (bf16[64,1024]{1,0:T(8,128)(2,1)S(1)}, bf16[64,1024]{1,0:T(8,128)(2,1)S(1)}) fusion(bf16[64,1024]{1,0:T(8,128)(2,1)S(1)} %fusion.91, pred[]{:T(512)S(6)} %eq.78, bf16[64,2816]{1,0:T(8,128)(2,1)S(1)} %collective-permute-done.13, bf16[1,2816,1024]{2,1,0:T(8,128)(2,1)} %param.27), kind=kOutput, calls=%fused_computation.88 | convolution fusion | flops 369229824 | bytes 6520833 | tf_op jit(solution)/shard_map/dot_general | solution.py:170
  196.3 3.6 %all-to-all-start.5 = ((bf16[8,8,1024]{2,1,0:T(8,128)(2,1)}), bf16[8,8,1024]{2,1,0:T(8,128)(2,1)S(1)}, u32[]{:S(2)}, u32[]{:S(2)}) async-start(bf16[8,8,1024]{2,1,0:T(8,128)(2,1)} %fusion.97), calls=%async_computation.5 | async-start | bytes 262144 | tf_op jit(solution)/shard_map/all_to_all | solution.py:183
  200.1 7.1 %all-to-all-done.5 = bf16[8,8,1024]{2,1,0:T(8,128)(2,1)S(1)} async-done(((bf16[8,8,1024]{2,1,0:T(8,128)(2,1)}), bf16[8,8,1024]{2,1,0:T(8,128)(2,1)S(1)}, u32[]{:S(2)}, u32[]{:S(2)}) %all-to-all-start.5) | async-done | bytes 131104 | tf_op jit(solution)/shard_map/all_to_all | solution.py:183
  (106 shorter events, 58.2 us)
Async XLA Ops:
  18.2 4.7 %collective-permute-start = (f32[128]{0:T(128)S(1)}, f32[128]{0:T(128)S(1)}, u32[]{:S(2)}, u32[]{:S(2)}) collective-permute-start(f32[128]{0:T(128)S(1)} %reduce_sum.56), channel_id=1, source_target_pairs={{0,1},{1,0},{2,3},{3,2},{4,5},{5,4},{6,7},{7,6},{8,9},{9,8},{10,11... | collective-permute-start | bytes 1544 | tf_op jit(solution)/shard_map/ppermute | solution.py:264
  25.1 14.6 %all-to-all-start = ((bf16[8,16,1024]{2,1,0:T(8,128)(2,1)}), bf16[8,16,1024]{2,1,0:T(8,128)(2,1)S(1)}, u32[]{:S(2)}, u32[]{:S(2)}) async-start(bf16[8,16,1024]{2,1,0:T(8,128)(2,1)} %bitcast.7), calls=%async_computation | async-start | bytes 524288 | tf_op jit(solution)/shard_map/all_to_all | solution.py:183
  39.7 1.5 collective-permute-start.1
  49.3 19.3 %collective-permute-start.6 = (bf16[128,2816]{1,0:T(8,128)(2,1)}, bf16[128,2816]{1,0:T(8,128)(2,1)}, u32[]{:S(2)}, u32[]{:S(2)}) collective-permute-start(bf16[128,2816]{1,0:T(8,128)(2,1)} %fusion.48), channel_id=1, source_target_pairs={{0,1},{1,0},{2,3},{3,2},{4,5},{5,4},{6,7},{7,6},{8,9},{9,8},{10,11... | collective-permute-start | bytes 2162696 | tf_op jit(solution)/shard_map/ppermute | solution.py:224
  50.6 12.7 %all-to-all-start.1 = ((bf16[8,16,1024]{2,1,0:T(8,128)(2,1)}), bf16[8,16,1024]{2,1,0:T(8,128)(2,1)S(1)}, u32[]{:S(2)}, u32[]{:S(2)}) async-start(bf16[8,16,1024]{2,1,0:T(8,128)(2,1)} %bitcast.11), calls=%async_computation.1 | async-start | bytes 524288 | tf_op jit(solution)/shard_map/all_to_all | solution.py:183
  55.0 28.2 %collective-permute-start.7 = (bf16[128,2816]{1,0:T(8,128)(2,1)S(1)}, bf16[128,2816]{1,0:T(8,128)(2,1)}, u32[]{:S(2)}, u32[]{:S(2)}) collective-permute-start(bf16[128,2816]{1,0:T(8,128)(2,1)S(1)} %fusion.54), channel_id=1, source_target_pairs={{0,1},{1,0},{2,3},{3,2},{4,5},{5,4},{6,7},{7,6},{8,9},{9,8},{10,11... | collective-permute-start | bytes 2162696 | tf_op jit(solution)/shard_map/ppermute | solution.py:225
  63.3 10.2 %collective-permute-start.2 = (bf16[128,1024]{1,0:T(8,128)(2,1)S(1)}, bf16[128,1024]{1,0:T(8,128)(2,1)S(1)}, u32[]{:S(2)}, u32[]{:S(2)}) collective-permute-start(bf16[128,1024]{1,0:T(8,128)(2,1)S(1)} %bitcast.177), channel_id=1, source_target_pairs={{0,2},{2,0},{4,6},{6,4},{8,10},{10,8},{12,14},{14,12},{16,18},{18,... | collective-permute-start | bytes 786440 | tf_op jit(solution)/shard_map/ppermute | solution.py:214
  79.7 10.8 %all-to-all-start.3 = ((bf16[8,8,1024]{2,1,0:T(8,128)(2,1)}), bf16[8,8,1024]{2,1,0:T(8,128)(2,1)S(1)}, u32[]{:S(2)}, u32[]{:S(2)}) async-start(bf16[8,8,1024]{2,1,0:T(8,128)(2,1)} %bitcast.20), calls=%async_computation.3 | async-start | bytes 262144 | tf_op jit(solution)/shard_map/all_to_all | solution.py:183
  87.6 19.1 %collective-permute-start.8 = (bf16[128,2816]{1,0:T(8,128)(2,1)S(1)}, bf16[128,2816]{1,0:T(8,128)(2,1)S(1)}, u32[]{:S(2)}, u32[]{:S(2)}) collective-permute-start(bf16[128,2816]{1,0:T(8,128)(2,1)S(1)} %multiply_convert_fusion), channel_id=1, source_target_pairs={{0,1},{1,0},{2,3},{3,2},{4,5},{5,4},{6,7},{7,6},{8,9},{9,8},{10,11... | collective-permute-start | bytes 2162696 | tf_op jit(solution)/shard_map/ppermute | solution.py:227
  90.5 5.8 %collective-permute-start.10 = (bf16[64,1024]{1,0:T(8,128)(2,1)S(1)}, bf16[64,1024]{1,0:T(8,128)(2,1)S(1)}, u32[]{:S(2)}, u32[]{:S(2)}) collective-permute-start(bf16[64,1024]{1,0:T(8,128)(2,1)S(1)} %bitcast.191), channel_id=1, source_target_pairs={{0,2},{2,0},{4,6},{6,4},{8,10},{10,8},{12,14},{14,12},{16,18},{18,... | collective-permute-start | bytes 393224 | tf_op jit(solution)/shard_map/ppermute | solution.py:214
  94.2 28.0 %collective-permute-start.3 = (bf16[128,2816]{1,0:T(8,128)(2,1)}, bf16[128,2816]{1,0:T(8,128)(2,1)S(1)}, u32[]{:S(2)}, u32[]{:S(2)}) collective-permute-start(bf16[128,2816]{1,0:T(8,128)(2,1)} %fusion.51), channel_id=1, source_target_pairs={{0,1},{1,0},{2,3},{3,2},{4,5},{5,4},{6,7},{7,6},{8,9},{9,8},{10,11... | collective-permute-start | bytes 2162696 | tf_op jit(solution)/shard_map/ppermute | solution.py:224
  95.4 42.3 %collective-permute-start.4 = (bf16[128,2816]{1,0:T(8,128)(2,1)}, bf16[128,2816]{1,0:T(8,128)(2,1)S(1)}, u32[]{:S(2)}, u32[]{:S(2)}) collective-permute-start(bf16[128,2816]{1,0:T(8,128)(2,1)} %fusion.57), channel_id=1, source_target_pairs={{0,1},{1,0},{2,3},{3,2},{4,5},{5,4},{6,7},{7,6},{8,9},{9,8},{10,11... | collective-permute-start | bytes 2162696 | tf_op jit(solution)/shard_map/ppermute | solution.py:225
  100.8 69.7 %collective-permute-start.12 = (bf16[64,2816]{1,0:T(8,128)(2,1)}, bf16[64,2816]{1,0:T(8,128)(2,1)}, u32[]{:S(2)}, u32[]{:S(2)}) collective-permute-start(bf16[64,2816]{1,0:T(8,128)(2,1)} %fusion.69), channel_id=1, source_target_pairs={{0,1},{1,0},{2,3},{3,2},{4,5},{5,4},{6,7},{7,6},{8,9},{9,8},{10,11... | collective-permute-start | bytes 1081352 | tf_op jit(solution)/shard_map/ppermute | solution.py:225
  103.8 49.4 %collective-permute-start.11 = (bf16[64,2816]{1,0:T(8,128)(2,1)}, bf16[64,2816]{1,0:T(8,128)(2,1)S(1)}, u32[]{:S(2)}, u32[]{:S(2)}) collective-permute-start(bf16[64,2816]{1,0:T(8,128)(2,1)} %fusion.66), channel_id=1, source_target_pairs={{0,1},{1,0},{2,3},{3,2},{4,5},{5,4},{6,7},{7,6},{8,9},{9,8},{10,11... | collective-permute-start | bytes 1081352 | tf_op jit(solution)/shard_map/ppermute | solution.py:224
  107.8 29.9 %slice-start.6 = ((s8[5767168]{0:T(1024)(128)(4,1)}), s8[4194304]{0:T(1024)(128)(4,1)S(1)}, s32[]{:S(2)}) async-start(s8[5767168]{0:T(1024)(128)(4,1)} %bitcast.175), calls=%async_computation.12 | async-start | bytes 8388608
  107.8 29.8 %slice-start.7 = ((s8[5767168]{0:T(1024)(128)(4,1)}), s8[1572864]{0:T(1024)(128)(4,1)S(1)}, s32[]{:S(2)}) async-start(s8[5767168]{0:T(1024)(128)(4,1)} %bitcast.175), calls=%async_computation.13 | async-start | bytes 3145728
  107.8 32.4 %collective-permute-start.9 = (bf16[128,1024]{1,0:T(8,128)(2,1)S(1)}, bf16[128,1024]{1,0:T(8,128)(2,1)S(1)}, u32[]{:S(2)}, u32[]{:S(2)}) collective-permute-start(bf16[128,1024]{1,0:T(8,128)(2,1)S(1)} %get-tuple-element.33), channel_id=1, source_target_pairs={{0,2},{2,0},{4,6},{6,4},{8,10},{10,8},{12,14},{14,12},{16,18},{18,... | collective-permute-start | bytes 786440 | tf_op jit(solution)/shard_map/ppermute | solution.py:235
  138.9 27.9 %collective-permute-start.5 = (bf16[128,2816]{1,0:T(8,128)(2,1)S(1)}, bf16[128,2816]{1,0:T(8,128)(2,1)S(1)}, u32[]{:S(2)}, u32[]{:S(2)}) collective-permute-start(bf16[128,2816]{1,0:T(8,128)(2,1)S(1)} %multiply_convert_fusion.1), channel_id=1, source_target_pairs={{0,1},{1,0},{2,3},{3,2},{4,5},{5,4},{6,7},{7,6},{8,9},{9,8},{10,11... | collective-permute-start | bytes 2162696 | tf_op jit(solution)/shard_map/ppermute | solution.py:227
  141.1 20.2 %all-to-all-start.2 = ((bf16[8,16,1024]{2,1,0:T(8,128)(2,1)}), bf16[8,16,1024]{2,1,0:T(8,128)(2,1)S(1)}, u32[]{:S(2)}, u32[]{:S(2)}) async-start(bf16[8,16,1024]{2,1,0:T(8,128)(2,1)} %bitcast.14), calls=%async_computation.2 | async-start | bytes 524288 | tf_op jit(solution)/shard_map/all_to_all | solution.py:183
  170.4 5.3 %collective-permute-start.14 = (bf16[128,1024]{1,0:T(8,128)(2,1)S(1)}, bf16[128,1024]{1,0:T(8,128)(2,1)S(1)}, u32[]{:S(2)}, u32[]{:S(2)}) collective-permute-start(bf16[128,1024]{1,0:T(8,128)(2,1)S(1)} %get-tuple-element.35), channel_id=1, source_target_pairs={{0,2},{2,0},{4,6},{6,4},{8,10},{10,8},{12,14},{14,12},{16,18},{18,... | collective-permute-start | bytes 786440 | tf_op jit(solution)/shard_map/ppermute | solution.py:235
  174.3 10.9 %collective-permute-start.13 = (bf16[64,2816]{1,0:T(8,128)(2,1)S(1)}, bf16[64,2816]{1,0:T(8,128)(2,1)S(1)}, u32[]{:S(2)}, u32[]{:S(2)}) collective-permute-start(bf16[64,2816]{1,0:T(8,128)(2,1)S(1)} %multiply_convert_fusion.2), channel_id=1, source_target_pairs={{0,1},{1,0},{2,3},{3,2},{4,5},{5,4},{6,7},{7,6},{8,9},{9,8},{10,11... | collective-permute-start | bytes 1081352 | tf_op jit(solution)/shard_map/ppermute | solution.py:227
  176.5 14.0 %all-to-all-start.4 = ((bf16[8,16,1024]{2,1,0:T(8,128)(2,1)}), bf16[8,16,1024]{2,1,0:T(8,128)(2,1)S(1)}, u32[]{:S(2)}, u32[]{:S(2)}) async-start(bf16[8,16,1024]{2,1,0:T(8,128)(2,1)} %bitcast.22), calls=%async_computation.4 | async-start | bytes 524288 | tf_op jit(solution)/shard_map/all_to_all | solution.py:183
  194.2 1.4 collective-permute-start.15
  196.3 10.9 %all-to-all-start.5 = ((bf16[8,8,1024]{2,1,0:T(8,128)(2,1)}), bf16[8,8,1024]{2,1,0:T(8,128)(2,1)S(1)}, u32[]{:S(2)}, u32[]{:S(2)}) async-start(bf16[8,8,1024]{2,1,0:T(8,128)(2,1)} %fusion.97), calls=%async_computation.5 | async-start | bytes 262144 | tf_op jit(solution)/shard_map/all_to_all | solution.py:183
  (11 other events, 182.1 us)
